TPU v7x, 256 devices: a whole 4x4x8 slice. The times are simulated.
256 devices in a mesh: row: 64 (over z, y, core), col: 4 (over x).
Axes of the slice: x: 4, y: 4, z: 8, core: 2. Of those that a mesh axis runs over, the one named last changes fastest.
Arguments:
- design: bfloat16 [524288, 512], P('row', 'col'), may hold values from -6 to 6
- row_signs: int32 [524288], P('row'), may hold values from -1 to 1, as said below
- sampled: int32 [64, 256], P('row'), may hold values from 0 to 8191, as said below
Outputs:
- sketch: float32 [16384, 512], P('row', 'col')
- sketch_gram: float32 [512, 512], P('row', 'col')
Inputs may be any that keep to these rules, and one draw needn't show every extreme that they name: `row_signs`: each entry is -1 or +1. `sampled`: each row is non-decreasing; offsets may repeat; in each row, entries s * 4 to (s + 1) * 4 - 1 lie in s * 128 to (s + 1) * 128 - 1, for every s below 64.
All inputs are finite; a program needn't handle non-finite values.
Results may differ from a plain program's by a relative error of at most 0.0003.
Values sent between devices are 32-bit elements; how exact they have to be, the bound alone decides.
A program may use at most 64 MiB of HBM per device.

v0:
```python
import jax
import jax.numpy as jnp
from jax import lax
from jax.sharding import PartitionSpec as P


def partner_2(value, axis, stride):
    return lax.ppermute(value, axis, [(i, i ^ 1 << stride) for i in range(lax.axis_size(axis))])


def hadamard(order):
    index = jnp.arange(order, dtype=jnp.int32)
    both = index[:, None] & index[None, :]
    parity = jnp.zeros((order, order), jnp.int32)
    for place in range(max(order.bit_length() - 1, 0)):
        parity = parity ^ both >> place & 1
    return (1 - 2 * parity).astype(jnp.float32)


def on_device(design, row_signs, sampled):
    local_rows, col_width = design.shape
    devices = lax.axis_size("row")
    scale = float(devices * local_rows) ** (-0.5)
    field = design.astype(jnp.float32) * row_signs.astype(jnp.float32)[:, None]
    field = field.reshape(local_rows // 128, 128, col_width)
    field = jnp.einsum(
        "ab,bjc->ajc", hadamard(local_rows // 128), field, precision=lax.Precision.HIGHEST
    )
    field = jnp.einsum("ij,ajc->aic", hadamard(128), field, precision=lax.Precision.HIGHEST)
    field = field.reshape(local_rows, col_width)
    my_index = lax.axis_index("row")
    for place in range(devices.bit_length() - 1):
        partner = partner_2(field, "row", place)
        is_upper = my_index >> place & 1 == 1
        field = jnp.where(is_upper, partner - field, field + partner)
    picked = field[sampled[0]] * scale
    all_columns = lax.all_gather(picked, "col", axis=1, tiled=True)
    total = float(picked.shape[0] * devices)
    gram = lax.psum_scatter(
        jnp.dot(
            all_columns.T,
            picked,
            precision=lax.Precision.HIGHEST,
            preferred_element_type=jnp.float32,
        )
        / total,
        "row",
        scatter_dimension=0,
        tiled=True,
    )
    return (picked, gram)


def solution(mesh):
    return jax.shard_map(
        on_device,
        mesh=mesh,
        in_specs=(P("row", "col"), P("row"), P("row", None)),
        out_specs=(P("row", "col"), P("row", "col")),
        check_vma=False,
    )
```

profile of v0, /device:TPU:1, one launch (start us, length us, event | category | flops | bytes accessed | tf_op | source)
XLA Modules:
  0.0 918.6 jit_solution(2463012365542698854)
XLA Ops:
  7.2 0.0 all-reduce.3.cloned.1.call-start
  7.2 0.8 convert_element_type.14
  8.0 4.6 convert_multiply_fusion
  12.5 6.2 fusion.2
  18.8 9.0 fusion
  27.7 3.2 collective-permute-start
  31.0 7.1 collective-permute-done
  38.1 5.8 add_select_fusion.5
  44.0 0.0 collective-permute-start.1
  44.0 92.1 %collective-permute-done.1 = f32[8192,128]{1,0:T(8,128)} collective-permute-done((f32[8192,128]{1,0:T(8,128)}, f32[8192,128]{1,0:T(8,128)}, u32[]{:S(2)}, u32[]{:S(2)}) %collective-permute-start.1) | collective-permute-done | bytes 4194336 | tf_op jit(solution)/shard_map/ppermute | solution.py:8
  136.1 5.8 add_select_fusion.4
  141.9 1.2 collective-permute-start.2
  143.1 91.5 %collective-permute-done.2 = f32[8192,128]{1,0:T(8,128)} collective-permute-done((f32[8192,128]{1,0:T(8,128)}, f32[8192,128]{1,0:T(8,128)}, u32[]{:S(2)}, u32[]{:S(2)}) %collective-permute-start.2) | collective-permute-done | bytes 4194336 | tf_op jit(solution)/shard_map/ppermute | solution.py:8
  234.6 5.8 add_select_fusion.3
  240.4 0.0 collective-permute-start.3
  240.4 90.3 %collective-permute-done.3 = f32[8192,128]{1,0:T(8,128)} collective-permute-done((f32[8192,128]{1,0:T(8,128)}, f32[8192,128]{1,0:T(8,128)}, u32[]{:S(2)}, u32[]{:S(2)}) %collective-permute-start.3) | collective-permute-done | bytes 4194336 | tf_op jit(solution)/shard_map/ppermute | solution.py:8
  330.7 5.8 add_select_fusion.2
  336.5 1.6 collective-permute-start.4
  338.1 0.0 copy-start.1
  338.1 181.8 %collective-permute-done.4 = f32[8192,128]{1,0:T(8,128)} collective-permute-done((f32[8192,128]{1,0:T(8,128)}, f32[8192,128]{1,0:T(8,128)}, u32[]{:S(2)}, u32[]{:S(2)}) %collective-permute-start.4) | collective-permute-done | bytes 4194336 | tf_op jit(solution)/shard_map/ppermute | solution.py:8
  519.9 5.8 add_select_fusion.1
  525.7 4.9 collective-permute-start.5
  530.6 0.0 copy-done.1
  530.6 0.0 copy-start.2
  530.6 181.2 %collective-permute-done.5 = f32[8192,128]{1,0:T(8,128)} collective-permute-done((f32[8192,128]{1,0:T(8,128)}, f32[8192,128]{1,0:T(8,128)}, u32[]{:S(2)}, u32[]{:S(2)}) %collective-permute-start.5) | collective-permute-done | bytes 4194336 | tf_op jit(solution)/shard_map/ppermute | solution.py:8
  711.8 5.8 add_select_fusion
  717.7 2.9 gather_fusion
  720.6 0.0 copy-start
  720.6 10.6 %all_gather.3 = f32[256,512]{1,0:T(8,128)S(1)} all-gather(f32[256,128]{1,0:T(8,128)S(1)} %broadcast_multiply_fusion), channel_id=1, replica_groups=mesh['row'=64,'col'=4] {'col'}, dimensions={1}, use_global_device_ids=true | all-gather | bytes 655360 | tf_op jit(solution)/shard_map/all_gather | solution.py:37
  731.2 1.7 convolution_multiply_fusion
  733.0 0.0 all-reduce.3.cloned.1.call-update
  733.0 0.0 copy-done.2
  733.0 0.6 dynamic-slice
  734.2 176.2 %all-reduce.3.cloned.1.call-done = f32[512,128]{1,0:T(8,128)} async-done(((f32[512,128]{1,0:T(8,128)}), f32[512,128]{1,0:T(8,128)}) %all-reduce.3.cloned.1.call-update) | async-done | bytes 262160
  910.5 1.3 constant_dynamic-slice_fusion
  911.8 0.0 copy-done
  (3 shorter events, 0.0 us)
Async XLA Ops:
  7.2 903.3 %all-reduce.3.cloned.1.call-start = ((), (), s32[]{:S(2)}) async-start(), calls=%async_computation | async-start | bytes 524288
  27.7 10.4 %collective-permute-start = (f32[8192,128]{1,0:T(8,128)}, f32[8192,128]{1,0:T(8,128)}, u32[]{:S(2)}, u32[]{:S(2)}) collective-permute-start(f32[8192,128]{1,0:T(8,128)} %bitcast.4), channel_id=1, source_target_pairs={{0,4},{4,0},{8,12},{12,8},{16,20},{20,16},{24,28},{28,24},{32,36},... | collective-permute-start | bytes 12582920 | tf_op jit(solution)/shard_map/ppermute | solution.py:8
  44.0 92.1 %collective-permute-start.1 = (f32[8192,128]{1,0:T(8,128)}, f32[8192,128]{1,0:T(8,128)}, u32[]{:S(2)}, u32[]{:S(2)}) collective-permute-start(f32[8192,128]{1,0:T(8,128)} %add_select_fusion.5), channel_id=1, source_target_pairs={{0,8},{4,12},{8,0},{12,4},{16,24},{20,28},{24,16},{28,20},{32,40},... | collective-permute-start | bytes 12582920 | tf_op jit(solution)/shard_map/ppermute | solution.py:8
  141.9 92.7 %collective-permute-start.2 = (f32[8192,128]{1,0:T(8,128)}, f32[8192,128]{1,0:T(8,128)}, u32[]{:S(2)}, u32[]{:S(2)}) collective-permute-start(f32[8192,128]{1,0:T(8,128)} %add_select_fusion.4), channel_id=1, source_target_pairs={{0,16},{4,20},{8,24},{12,28},{16,0},{20,4},{24,8},{28,12},{32,48},... | collective-permute-start | bytes 12582920 | tf_op jit(solution)/shard_map/ppermute | solution.py:8
  240.4 90.3 %collective-permute-start.3 = (f32[8192,128]{1,0:T(8,128)}, f32[8192,128]{1,0:T(8,128)}, u32[]{:S(2)}, u32[]{:S(2)}) collective-permute-start(f32[8192,128]{1,0:T(8,128)} %add_select_fusion.3), channel_id=1, source_target_pairs={{0,32},{4,36},{8,40},{12,44},{16,48},{20,52},{24,56},{28,60},{32,0... | collective-permute-start | bytes 12582920 | tf_op jit(solution)/shard_map/ppermute | solution.py:8
  336.5 183.3 %collective-permute-start.4 = (f32[8192,128]{1,0:T(8,128)}, f32[8192,128]{1,0:T(8,128)}, u32[]{:S(2)}, u32[]{:S(2)}) collective-permute-start(f32[8192,128]{1,0:T(8,128)} %add_select_fusion.2), channel_id=1, source_target_pairs={{0,64},{4,68},{8,72},{12,76},{16,80},{20,84},{24,88},{28,92},{32,9... | collective-permute-start | bytes 12582920 | tf_op jit(solution)/shard_map/ppermute | solution.py:8
  338.1 192.5 %copy-start.1 = (s32[1,256]{1,0:T(1,128)S(1)}, s32[1,256]{1,0:T(1,128)}, u32[]{:S(2)}) copy-start(s32[1,256]{1,0:T(1,128)} %param.5) | copy-start | bytes 3076
  525.7 186.1 %collective-permute-start.5 = (f32[8192,128]{1,0:T(8,128)}, f32[8192,128]{1,0:T(8,128)}, u32[]{:S(2)}, u32[]{:S(2)}) collective-permute-start(f32[8192,128]{1,0:T(8,128)} %add_select_fusion.1), channel_id=1, source_target_pairs={{0,128},{4,132},{8,136},{12,140},{16,144},{20,148},{24,152},{28,15... | collective-permute-start | bytes 12582920 | tf_op jit(solution)/shard_map/ppermute | solution.py:8
  530.6 202.4 %copy-start.2 = (u32[256]{0:T(256)S(1)}, u32[256]{0:T(256)}, u32[]{:S(2)}) copy-start(u32[256]{0:T(256)} %constant.6) | copy-start | bytes 3076
  720.6 191.2 %copy-start = (f32[256,128]{1,0:T(8,128)}, f32[256,128]{1,0:T(8,128)S(1)}, u32[]{:S(2)}) copy-start(f32[256,128]{1,0:T(8,128)S(1)} %broadcast_multiply_fusion) | copy-start | bytes 393220
Sparse Core Ops, SparseCore 0:
  733.1 177.3 all-reduce.2
where the time goes:
time: 919 us
  waiting for transfers between devices  820 us (89%)
  other arithmetic  40.4 us (4%)
  matrix products  16.9 us (2%)
  between operations  14.7 us (2%)
  starting transfers between devices  10.9 us (1%)
  blocking collectives  10.6 us (1%)
    ppermute x6, waiting for transfers between devices, partner_2(): lax.ppermute(value, axis, [(i, i ^ 1 << stride) for i in range(lax.axis_s...  644 us
    unnamed x2, waiting for transfers between devices  176 us
    select_n x6, other arithmetic, on_device(): field = jnp.where(is_upper, partner - field, field + partner)  35.1 us
  transfers between devices with their start and end apart: 7, of which 7 were waited for; matrix products, arithmetic and copies ran while one was open for 0% of the time, Pallas kernels for 0%

commit v1 on v0

v1 whole, which is shorter than its diff:
```python
import functools

import jax
import jax.numpy as jnp
from jax import lax
from jax.experimental import pallas as pl
from jax.experimental.pallas import tpu as pltpu
from jax.sharding import PartitionSpec as P

MESH = pl.DeviceIdType.MESH
NZ, NY = 8, 4
F32, BF16 = jnp.float32, jnp.bfloat16
CHUNKS = 4
PAIRS = 16
PARTS = (("z", 0, 4), ("y", 0, 4), ("z", 1, 4), ("y", 1, 4))


def split(v):
    high = v.astype(BF16)
    return high, (v - high.astype(F32)).astype(BF16)


def parity_sign(v):
    return (1 - 2 * (((v >> 2) ^ (v >> 1) ^ v) & 1)).astype(F32)


class Part:
    def __init__(self, kind, refs):
        self.axis, self.longer, self.pairs = kind
        self.q, self.r1, self.f, self.r2, self.s1, self.v1, self.s2, self.v2 = refs


class Arm:
    def __init__(self, me, n, step, reach, own, recv, slot, send_sem, recv_sem, device, sent):
        self.me, self.n, self.step, self.reach, self.own = me, n, step, reach, own
        self.recv, self.slot, self.sent = recv, slot, sent
        self.send_sem, self.recv_sem = send_sem, recv_sem
        self.device = device(self.at(step))
        self.copies = {}

    def at(self, offset):
        return lax.rem(self.me + self.n + offset, self.n)

    def start(self, s):
        if not 1 <= s <= self.reach:
            return
        index = self.slot + s - 1
        source = self.own(self.at(self.step * self.reach)) if s == 1 else self.recv.at[index - 1]
        copy = pltpu.make_async_remote_copy(
            src_ref=source,
            dst_ref=self.recv.at[index],
            send_sem=self.send_sem.at[index],
            recv_sem=self.recv_sem.at[index],
            device_id=self.device,
            device_id_type=MESH,
        )
        copy.start()
        self.copies[s] = copy
        self.sent.append(copy)

    def take(self, s):
        if not 1 <= s <= self.reach:
            return
        self.copies[s].wait_recv()
        if s < self.reach:
            here = self.recv.at[self.slot + s - 1]
            here[...] = here[...] + self.own(self.at(self.step * (self.reach - s)))[...]
            self.start(s + 1)


def kernel(
    nx, x_hbm, sgn_ref, smp_ref, sk_out, g_out,
    x_v, own, out_t, in_t, sloc, sidx, signs, sk, sib, xg, gbuf, g1, g1s, g2,
    load_sem, t_send, t_recv, i_send, i_recv, j_send, j_recv, x_send, x_recv, o_send, o_recv,
    g_send, g_recv, h_send, h_recv, *part_refs,
):
    row, col = lax.axis_index("row"), lax.axis_index("col")
    c = lax.rem(row, 2)
    yc = lax.rem(row, 2 * NY)
    y = yc // 2
    z = row // (2 * NY)
    nyc = 2 * NY
    half = PAIRS * 2
    sent = []

    def at_yc(v):
        return (z * nyc + v, col)

    def at_z(v):
        return (v * nyc + yc, col)

    def at_y(v):
        return (z * nyc + v * 2 + c, col)

    sibling = (row + 1 - 2 * c, col)

    barrier = pltpu.get_barrier_semaphore()
    for k in range(1, nyc):
        pl.semaphore_signal(barrier, inc=1, device_id=at_yc(lax.rem(yc + k, nyc)), device_id_type=MESH)
    for k in range(1, NZ):
        pl.semaphore_signal(barrier, inc=1, device_id=at_z(lax.rem(z + k, NZ)), device_id_type=MESH)
    for k in range(1, nx):
        pl.semaphore_signal(barrier, inc=1, device_id=(row, lax.rem(col + k, nx)), device_id_type=MESH)

    step = half // CHUNKS
    loads = []
    for g in range(CHUNKS):
        for top in range(2):
            rows = pl.ds(top * half + g * step, step)
            load = pltpu.make_async_copy(x_hbm.at[rows], x_v.at[rows], load_sem.at[2 * g + top])
            load.start()
            loads.append(load)

    for h in range(2):
        sloc[h] = smp_ref[:, h * 128 : (h + 1) * 128] & 127
    sidx[z, pl.ds(yc, 1), :] = sloc[c]

    pl.semaphore_wait(barrier, nyc - 1 + NZ - 1 + nx - 1)

    to_plane = []
    for k in range(1, nyc):
        there = lax.rem(yc + k, nyc)
        copy = pltpu.make_async_remote_copy(
            src_ref=sloc.at[lax.rem(there, 2)],
            dst_ref=sidx.at[z, pl.ds(yc, 1), :],
            send_sem=i_send.at[k - 1],
            recv_sem=i_recv.at[k - 1],
            device_id=at_yc(there),
            device_id_type=MESH,
        )
        copy.start()
        to_plane.append(copy)
    sent += to_plane

    lane = lax.broadcasted_iota(jnp.int32, (128, 128), 1)
    eye = (lane == lax.broadcasted_iota(jnp.int32, (128, 128), 0)).astype(F32)
    flip = (1 - 2 * c).astype(F32)
    t_copies = []
    for g in range(CHUNKS):
        loads[2 * g].wait()
        loads[2 * g + 1].wait()

        def first(i, _):
            a = g * step + i
            d0 = (eye * sgn_ref[pl.ds(a, 1), :].astype(F32)).astype(BF16)
            d1 = (eye * (sgn_ref[pl.ds(half + a, 1), :].astype(F32) * flip)).astype(BF16)
            v0 = jnp.dot(d0, x_v[a], preferred_element_type=F32)
            v1 = jnp.dot(d1, x_v[half + a], preferred_element_type=F32)
            out_t[a] = v0 - v1
            own[a] = v0 + v1
            return 0

        lax.fori_loop(0, step, first, 0, unroll=4)
        rows = pl.ds(g * step, step)
        copy = pltpu.make_async_remote_copy(
            src_ref=out_t.at[rows],
            dst_ref=in_t.at[rows],
            send_sem=t_send.at[g],
            recv_sem=t_recv.at[g],
            device_id=sibling,
            device_id_type=MESH,
        )
        copy.start()
        t_copies.append(copy)
    sent += t_copies

    for copy in to_plane:
        copy.wait_recv()
    along_z = []
    for k in range(1, NZ):
        copy = pltpu.make_async_remote_copy(
            src_ref=sidx.at[z],
            dst_ref=sidx.at[z],
            send_sem=j_send.at[k - 1],
            recv_sem=j_recv.at[k - 1],
            device_id=at_z(lax.rem(z + k, NZ)),
            device_id_type=MESH,
        )
        copy.start()
        along_z.append(copy)
    sent += along_z

    def transform(ref):
        def body(i, _):
            rows = pl.ds(pl.multiple_of(i * 8, 8), 8)
            v = [ref[a, rows, :] for a in range(half)]
            place = 1
            while place < half:
                for a in range(half):
                    if not a & place:
                        v[a], v[a | place] = v[a] + v[a | place], v[a] - v[a | place]
                place *= 2
            for a in range(half):
                ref[a, rows, :] = v[a]
            return 0

        lax.fori_loop(0, 16, body, 0)

    transform(own)

    for copy in along_z:
        copy.wait_recv()
    nb = NZ * nyc
    table = sidx[...].reshape(nb, 128).astype(F32)
    if nb < 128:
        table = jnp.concatenate([table, jnp.zeros((128 - nb, 128), F32)], axis=0)
    table = table.T.astype(jnp.int32)
    for bz in range(NZ):
        for by in range(NY):
            chip = parity_sign(bz & z) * parity_sign(by & y)
            rows = []
            for bc in range(2):
                b = bz * nyc + by * 2 + bc
                index = jnp.broadcast_to(table[:, b : b + 1], (128, 128))
                odd = (lax.population_count(index & lane) & 1).astype(F32)
                gain = chip * flip if bc else chip
                rows.append((gain - (2 * gain) * odd).reshape(PAIRS, 8, 128))
            mine = jnp.concatenate(rows, axis=1).astype(BF16)
            theirs = jnp.concatenate([rows[0], -rows[1]], axis=1).astype(BF16)
            first_pair = 0
            for axis, _, pairs in PARTS:
                place = bz * NY + by if axis == "z" else by * NZ + bz
                here = slice(first_pair, first_pair + pairs)
                signs[here, place * 16 : place * 16 + 16, :128] = mine[here]
                signs[here, place * 16 : place * 16 + 16, 128:] = theirs[here]
                first_pair += pairs

    for copy in t_copies:
        copy.wait_recv()
    transform(in_t)

    chips = NZ * NY
    lower = lax.broadcasted_iota(jnp.int32, (chips * 16, 128), 0) % 8 < 4
    parts, arms = [], []
    first_pair = 0
    for number, kind in enumerate(PARTS):
        part = Part(kind, part_refs[8 * number : 8 * number + 8])
        parts.append(part)
        n1, n2 = (NZ, NY) if part.axis == "z" else (NY, NZ)

        def product(i, _):
            p = first_pair + i
            field = jnp.concatenate(
                [
                    jnp.concatenate([own[2 * p], own[2 * p + 1]], axis=1),
                    jnp.concatenate([in_t[2 * p], in_t[2 * p + 1]], axis=1),
                ],
                axis=0,
            )
            high, low = split(field)
            both = jnp.dot(signs[p], high, preferred_element_type=F32) + jnp.dot(
                signs[p], low, preferred_element_type=F32
            )
            value = jnp.where(lower, both[:, :128], both[:, 128:])
            part.q[:, :, i] = value.reshape(n1, n2, 2, 8, 128)
            return 0

        lax.fori_loop(0, part.pairs, product, 0)
        first_pair += part.pairs
        me, device = (z, at_z) if part.axis == "z" else (y, at_y)
        long, short = n1 // 2, n1 - 1 - n1 // 2
        up, down = (short, long) if part.longer else (long, short)
        own_block = functools.partial(lambda q, t: q.at[t], part.q)
        args = (own_block, part.r1)
        part.up = Arm(me, n1, 1, up, *args, 0, part.s1, part.v1, device, sent)
        part.down = Arm(me, n1, -1, down, *args, up, part.s1, part.v1, device, sent)
        part.reach = long
        part.up.start(1)
        part.down.start(1)

    def turn(part):
        part.up.take(part.up.reach)
        part.down.take(part.down.reach)
        total = part.q[part.up.me]
        if part.up.reach:
            total = total + part.r1[part.up.slot + part.up.reach - 1]
        if part.down.reach:
            total = total + part.r1[part.down.slot + part.down.reach - 1]
        part.f[...] = total
        n2 = NY if part.axis == "z" else NZ
        me, device = (y, at_y) if part.axis == "z" else (z, at_z)
        long, short = n2 // 2, n2 - 1 - n2 // 2
        up, down = (short, long) if part.longer else (long, short)
        own_block = functools.partial(lambda f, t: f.at[t], part.f)
        args = (own_block, part.r2)
        part.up2 = Arm(me, n2, 1, up, *args, 0, part.s2, part.v2, device, sent)
        part.down2 = Arm(me, n2, -1, down, *args, up, part.s2, part.v2, device, sent)
        part.reach2 = long
        part.up2.start(1)
        part.down2.start(1)

    scale = float(8192 * NZ * nyc) ** (-0.5)
    x_copies = []

    def finish(part, number):
        part.up2.take(part.up2.reach)
        part.down2.take(part.down2.reach)
        total = part.f[part.up2.me]
        if part.up2.reach:
            total = total + part.r2[part.up2.slot + part.up2.reach - 1]
        if part.down2.reach:
            total = total + part.r2[part.down2.slot + part.down2.reach - 1]
        first = sum(kind[2] for kind in PARTS[:number])
        here = pl.ds(first, part.pairs)
        sk[:, here] = jnp.swapaxes(total * scale, 0, 1)
        for k in range(1, nx):
            copy = pltpu.make_async_remote_copy(
                src_ref=sk.at[:, here],
                dst_ref=xg.at[k - 1, :, here],
                send_sem=x_send.at[k - 1, number],
                recv_sem=x_recv.at[k - 1, number],
                device_id=(row, lax.rem(col + k, nx)),
                device_id_type=MESH,
            )
            copy.start()
            x_copies.append((k, copy))
            sent.append(copy)

    def advance(part, s):
        if s < part.up.reach:
            part.up.take(s)
        if s < part.down.reach:
            part.down.take(s)

    def advance2(part, s):
        if s < part.up2.reach:
            part.up2.take(s)
        if s < part.down2.reach:
            part.down2.take(s)

    z_parts = [p for p in parts if p.axis == "z"]
    y_parts = [p for p in parts if p.axis == "y"]
    for s in range(1, NZ // 2):
        for part in z_parts:
            advance(part, s)
        for part in y_parts:
            advance(part, s)
    for part in y_parts:
        turn(part)
    for part in z_parts:
        turn(part)
    for s in range(1, NZ // 2):
        for part in y_parts:
            advance2(part, s)
        for part in z_parts:
            advance2(part, s)
    for part in z_parts + y_parts:
        finish(part, parts.index(part))

    swap = pltpu.make_async_remote_copy(
        src_ref=sk.at[1 - c],
        dst_ref=sib,
        send_sem=o_send.at[0],
        recv_sem=o_recv.at[0],
        device_id=sibling,
        device_id_type=MESH,
    )
    swap.start()
    sent.append(swap)
    sk_out[c] = sk[c]

    gr = nx * 128 // nb
    per_x = NZ // nx
    mine_high, mine_low = split(sk[...].reshape(256, 128))
    for k in range(nx):
        if k:
            for which, copy in x_copies:
                if which == k:
                    copy.wait_recv()
            high, low = split(xg[k - 1].reshape(256, 128))
        else:
            high, low = mine_high, mine_low
        dims = (((0,), (0,)), ((), ()))
        block = (
            lax.dot_general(high, mine_high, dims, preferred_element_type=F32)
            + lax.dot_general(high, mine_low, dims, preferred_element_type=F32)
            + lax.dot_general(low, mine_high, dims, preferred_element_type=F32)
        ).reshape(per_x, nyc, gr, 128)
        from_x = lax.rem(col + nx - k, nx)
        for i in range(per_x):
            gbuf[:, from_x * per_x + i] = block[i]

    in_plane = []
    for k in range(1, nyc):
        there = lax.rem(yc + k, nyc)
        copy = pltpu.make_async_remote_copy(
            src_ref=gbuf.at[there],
            dst_ref=g1.at[k - 1],
            send_sem=g_send.at[k - 1],
            recv_sem=g_recv.at[k - 1],
            device_id=at_yc(there),
            device_id_type=MESH,
        )
        copy.start()
        in_plane.append(copy)
    sent += in_plane
    total = gbuf[yc]
    for k, copy in enumerate(in_plane):
        copy.wait_recv()
        total = total + g1[k]
    g1s[...] = total
    in_column = []
    for k in range(1, NZ):
        there = lax.rem(z + k, NZ)
        copy = pltpu.make_async_remote_copy(
            src_ref=g1s.at[there],
            dst_ref=g2.at[k - 1],
            send_sem=h_send.at[k - 1],
            recv_sem=h_recv.at[k - 1],
            device_id=at_z(there),
            device_id_type=MESH,
        )
        copy.start()
        in_column.append(copy)
    sent += in_column
    swap.wait_recv()
    sk_out[1 - c] = sib[...]
    total = g1s[z]
    for k, copy in enumerate(in_column):
        copy.wait_recv()
        total = total + g2[k]
    g_out[...] = total * (1.0 / float(256 * nb))
    for copy in sent:
        copy.wait_send()


def on_device(nx, design, row_signs, sampled):
    vm, dma = pltpu.VMEM, pltpu.SemaphoreType.DMA
    half = PAIRS * 2
    nyc = 2 * NY
    nb = NZ * nyc
    gr = nx * 128 // nb
    scratch = [
        vm((2 * half, 128, 128), BF16),
        vm((half, 128, 128), F32),
        vm((half, 128, 128), F32),
        vm((half, 128, 128), F32),
        vm((2, 1, 128), jnp.int32),
        vm((NZ, nyc, 128), jnp.int32),
        vm((PAIRS, NZ * NY * 16, 256), BF16),
        vm((2, PAIRS, 8, 128), F32),
        vm((PAIRS, 8, 128), F32),
        vm((max(nx - 1, 1), 2, PAIRS, 8, 128), F32),
        vm((nyc, NZ, gr, 128), F32),
        vm((nyc - 1, NZ, gr, 128), F32),
        vm((NZ, gr, 128), F32),
        vm((NZ - 1, gr, 128), F32),
        dma((2 * CHUNKS,)),
        dma((CHUNKS,)),
        dma((CHUNKS,)),
        dma((nyc - 1,)),
        dma((nyc - 1,)),
        dma((NZ - 1,)),
        dma((NZ - 1,)),
        dma((max(nx - 1, 1), len(PARTS))),
        dma((max(nx - 1, 1), len(PARTS))),
        dma((1,)),
        dma((1,)),
        dma((nyc - 1,)),
        dma((nyc - 1,)),
        dma((NZ - 1,)),
        dma((NZ - 1,)),
    ]
    for axis, _, pairs in PARTS:
        n1, n2 = (NZ, NY) if axis == "z" else (NY, NZ)
        scratch += [
            vm((n1, n2, pairs, 2, 8, 128), F32),
            vm((n1 - 1, n2, pairs, 2, 8, 128), F32),
            vm((n2, pairs, 2, 8, 128), F32),
            vm((n2 - 1, pairs, 2, 8, 128), F32),
            dma((n1 - 1,)),
            dma((n1 - 1,)),
            dma((n2 - 1,)),
            dma((n2 - 1,)),
        ]
    sketch, gram = pl.pallas_call(
        functools.partial(kernel, nx),
        out_shape=(
            jax.ShapeDtypeStruct((2, PAIRS, 8, 128), F32),
            jax.ShapeDtypeStruct((gr, 128), F32),
        ),
        in_specs=[
            pl.BlockSpec(memory_space=pl.ANY),
            pl.BlockSpec(memory_space=pltpu.VMEM),
            pl.BlockSpec(memory_space=pltpu.VMEM),
        ],
        out_specs=(pl.BlockSpec(memory_space=pltpu.VMEM), pl.BlockSpec(memory_space=pltpu.VMEM)),
        scratch_shapes=scratch,
        compiler_params=pltpu.CompilerParams(
            collective_id=0, has_side_effects=True, vmem_limit_bytes=48 * 1024 * 1024
        ),
    )(design.reshape(2 * half, 128, 128), row_signs.reshape(2 * half, 128), sampled)
    return sketch.reshape(256, 128), gram


def solution(mesh):
    return jax.shard_map(
        functools.partial(on_device, mesh.shape["col"]),
        mesh=mesh,
        in_specs=(P("row", "col"), P("row"), P("row", None)),
        out_specs=(P("row", "col"), P("row", "col")),
        check_vma=False,
    )
```

time: 919 us -> 78.5 us (0.09)
  waiting for transfers between devices: 820 us -> 0 us
  Pallas kernels: 0 us -> 73.3 us
  other arithmetic: 40.4 us -> 0 us
  matrix products: 16.9 us -> 0 us
  between operations: 14.7 us -> 0.65 us
  starting transfers between devices: 10.9 us -> 0 us
  blocking collectives: 10.6 us -> 0 us
    ppermute x6 -> x0, waiting for transfers between devices: 644 us -> none  [partner_2(): lax.ppermute(value, axis, [(i, i ^ 1 << stride) for i in range(lax.axis_s...]
    unnamed x2 -> x0, waiting for transfers between devices: 176 us -> none
    pallas_call x0 -> x1, Pallas kernels: none -> 73.3 us  [on_device(): pl.pallas_call(functools.partial(kernel, nx), out_shape=(jax.ShapeDtypeSt...]
    select_n x7 -> x0, other arithmetic: 35.1 us -> none  [the longest x6 35.1 us: on_device(): field = jnp.where(is_upper, partner - field, field + partner)]
    dot_general x3 -> x0, matrix products: 16.9 us -> none  [the longest x1 8.96 us: on_device(): jnp.einsum('ij,ajc->aic', hadamard(128), field, precision=lax.Precision.H...]
    ppermute x6 -> x0, starting transfers between devices: 10.9 us -> none  [partner_2(): lax.ppermute(value, axis, [(i, i ^ 1 << stride) for i in range(lax.axis_s...]
    all_gather x1 -> x0, blocking collectives: 10.6 us -> none  [on_device(): all_columns = lax.all_gather(picked, 'col', axis=1, tiled=True)]
  transfers between devices with their start and end apart: 7 -> 0, of which waited for: 7 -> 0; matrix products, arithmetic and copies ran while one was open for 0% -> 0% of each run, Pallas kernels for 0% -> 0%
where the time goes in v1:
time: 78.5 us; the launch traced here: 78.3 us
  Pallas kernels  73.3 us (93%)
  local copies, waits for them, and re-layouts  4.27 us (5%)
    pallas_call x1, Pallas kernels, on_device(): pl.pallas_call(functools.partial(kernel, nx), out_shape=(jax.ShapeDtypeSt...  73.3 us
    unnamed x8, local copies, waits for them, and re-layouts  4.27 us

profile of v1, /device:TPU:1, one launch (start us, length us, event | category | flops | bytes accessed | tf_op | source)
XLA Modules:
  0.0 78.3 jit_solution(7029613200195254351)
XLA Ops:
  0.6 0.0 copy-start
  0.6 1.6 %copy-done = bf16[8192,128]{1,0:T(8,128)(2,1)S(1)} copy-done((bf16[8192,128]{1,0:T(8,128)(2,1)S(1)}, bf16[8192,128]{1,0:T(8,128)(2,1)}, u32[]{:S(2)}) %copy-start) | copy-done | bytes 2097176
  2.2 0.0 copy-start.1
  2.2 0.8 copy-done.1
  3.0 0.0 copy-start.2
  3.0 0.7 copy-done.2
  3.7 73.3 %shard_map.50 = (f32[2,16,8,128]{3,2,1,0:T(8,128)S(1)}, f32[8,128]{1,0:T(8,128)S(1)}) custom-call(bf16[64,128,128]{2,1,0:T(8,128)(2,1)S(1)} %bitcast.3, s32[64,128]{1,0:T(8,128)S(1)} %bitcast.5, s32[1,256]{1,0:T(1,128)S(1)} %copy-done.2), custom_call_target="tpu_custom_call" | custom-call | tf_op jit(solution)/shard_map/pallas_call | solution.py:476
  77.0 0.7 copy.7
  77.7 0.6 copy.8
Async XLA Ops:
  0.6 1.6 %copy-start = (bf16[8192,128]{1,0:T(8,128)(2,1)S(1)}, bf16[8192,128]{1,0:T(8,128)(2,1)}, u32[]{:S(2)}) copy-start(bf16[8192,128]{1,0:T(8,128)(2,1)} %param.3) | copy-start | bytes 6291460
  2.2 0.8 copy-start.1
  3.0 0.7 copy-start.2

commit v2 on v0

v2 whole, which is shorter than its diff:
```python
import functools

import jax
import jax.numpy as jnp
from jax import lax
from jax.experimental import pallas as pl
from jax.experimental.pallas import tpu as pltpu
from jax.sharding import PartitionSpec as P

MESH = pl.DeviceIdType.MESH
NZ, NY = 8, 4
F32, BF16 = jnp.float32, jnp.bfloat16
CHUNKS = 4
PAIRS = 16
PARTS = (
    ("z", 2, 0, True),
    ("y", 2, 0, False),
    ("z", 2, 1, True),
    ("y", 2, 1, False),
    ("z", 2, 0, True),
    ("y", 2, 0, False),
    ("z", 2, 1, True),
    ("y", 2, 1, False),
)
ORDER = (
    (0, 1, 0, 1), (0, 1, 1, 1), (2, 1, 0, 1), (2, 1, 1, 1), (1, 1, 0, 1), (1, 1, 1, 1), (4, 1, 0, 1), (4, 1, 1, 1),
    (0, 1, 0, 2), (3, 1, 0, 1), (3, 1, 1, 1), (0, 1, 1, 2), (6, 1, 0, 1), (6, 1, 1, 1), (2, 1, 0, 2), (5, 1, 0, 1),
    (5, 1, 1, 1), (2, 1, 1, 2), (4, 1, 0, 2), (4, 1, 1, 2), (0, 1, 0, 3), (7, 1, 0, 1), (7, 1, 1, 1), (0, 1, 1, 3),
    (6, 1, 0, 2), (6, 1, 1, 2), (2, 1, 0, 3), (1, 1, 0, 2), (3, 1, 1, 2), (2, 1, 1, 3), (4, 1, 0, 3), (4, 1, 1, 3),
    (0, 1, 0, 4), (5, 1, 0, 2), (7, 1, 1, 2), (6, 1, 1, 3), (1, 2, 1, 1), (3, 2, 1, 1), (6, 1, 0, 3), (1, 2, 0, 1),
    (3, 2, 0, 1), (2, 1, 1, 4), (5, 2, 1, 1), (7, 2, 1, 1), (4, 1, 0, 4), (5, 2, 0, 1), (0, 2, 0, 1), (7, 2, 0, 1),
    (1, 2, 0, 2), (6, 1, 1, 4), (3, 2, 0, 2), (1, 2, 1, 2), (3, 2, 1, 2), (5, 2, 1, 2), (2, 2, 0, 1), (7, 2, 1, 2),
    (5, 2, 0, 2), (7, 2, 0, 2), (4, 2, 0, 1), (1, 2, 0, 3), (3, 2, 0, 3), (1, 2, 1, 3), (3, 2, 1, 3), (6, 2, 0, 1),
    (5, 2, 1, 3), (7, 2, 1, 3), (5, 2, 0, 3), (7, 2, 0, 3), (1, 2, 0, 4), (3, 2, 1, 4), (7, 2, 1, 4), (5, 2, 0, 4),
)


def split(v):
    high = v.astype(BF16)
    return high, (v - high.astype(F32)).astype(BF16)


class Arm:
    def __init__(self, me, n, step, reach, own, recv, slot, send_sem, recv_sem, device, sent):
        self.me, self.n, self.step, self.reach, self.own = me, n, step, reach, own
        self.recv, self.slot, self.sent = recv, slot, sent
        self.send_sem, self.recv_sem = send_sem, recv_sem
        self.device = device(self.at(step))
        self.copies = {}

    def at(self, offset):
        return lax.rem(self.me + self.n + offset, self.n)

    def start(self, s):
        if not 1 <= s <= self.reach:
            return
        index = self.slot + s - 1
        source = self.own(self.at(self.step * self.reach)) if s == 1 else self.recv.at[index - 1]
        copy = pltpu.make_async_remote_copy(
            src_ref=source,
            dst_ref=self.recv.at[index],
            send_sem=self.send_sem.at[index],
            recv_sem=self.recv_sem.at[index],
            device_id=self.device,
            device_id_type=MESH,
        )
        copy.start()
        self.copies[s] = copy
        self.sent.append(copy)

    def take(self, s):
        self.copies[s].wait_recv()
        if s < self.reach:
            here = self.recv.at[self.slot + s - 1]
            here[...] = here[...] + self.own(self.at(self.step * (self.reach - s)))[...]
            self.start(s + 1)


class Stage:
    def __init__(self, me, n, longer, direct, source, recv, send_sem, recv_sem, device, sent):
        self.me, self.source, self.recv = me, source, recv
        self.direct = []
        self.arms = []
        if direct:
            for k in range(1, n):
                there = lax.rem(me + k, n)
                copy = pltpu.make_async_remote_copy(
                    src_ref=source.at[there],
                    dst_ref=recv.at[k - 1],
                    send_sem=send_sem.at[k - 1],
                    recv_sem=recv_sem.at[k - 1],
                    device_id=device(there),
                    device_id_type=MESH,
                )
                copy.start()
                sent.append(copy)
                self.direct.append(copy)
            self.left = 1
            self.last = list(range(n - 1))
            return
        long, short = n // 2, n - 1 - n // 2
        up, down = (short, long) if longer else (long, short)
        own = lambda t: source.at[t]
        for step, reach, slot in ((1, up, 0), (-1, down, up)):
            self.arms.append(Arm(me, n, step, reach, own, recv, slot, send_sem, recv_sem, device, sent))
            self.arms[-1].start(1)
        self.left = n - 1
        self.last = [arm.slot + arm.reach - 1 for arm in self.arms if arm.reach]

    def take(self, direction, step):
        if self.direct:
            for copy in self.direct:
                copy.wait_recv()
        elif step <= self.arms[direction].reach:
            self.arms[direction].take(step)
        else:
            return False
        self.left -= 1
        return self.left == 0

    def total(self):
        value = self.source[self.me]
        for slot in self.last:
            value = value + self.recv[slot]
        return value


def kernel(
    nx, x_hbm, sgn_hbm, smp_hbm, sk_out, g_out,
    x_v, sgn_ref, smp_ref, own, out_t, in_t, sloc, sidx, table, signs0, signs1, sk, xg, gbuf, g2,
    load_sem, t_send, t_recv, i_send, i_recv, x_send, x_recv, h_send, h_recv, *part_refs,
):
    row, col = lax.axis_index("row"), lax.axis_index("col")
    c = lax.rem(row, 2)
    chip = row // 2
    y = lax.rem(chip, NY)
    z = chip // NY
    chips = NZ * NY
    half = PAIRS * 2
    sent = []

    rows_all = 2 * chips
    other = 1 - c

    def at_chip(v):
        return (v * 2 + c, col)

    def at_z(v):
        return at_chip(v * NY + y)

    def at_y(v):
        return at_chip(z * NY + v)

    def other_chip(k):
        return lax.rem(chip + k, chips)

    def other_row(k):
        return lax.rem(row + k, rows_all)

    def other_col(k):
        return lax.rem(col + k, nx)

    beside = row + 1 - 2 * c
    sibling = (beside, col)

    small = []
    for number, (source, target) in enumerate(((smp_hbm, smp_ref), (sgn_hbm, sgn_ref))):
        load = pltpu.make_async_copy(source, target, load_sem.at[2 * CHUNKS + number])
        load.start()
        small.append(load)
    step = half // CHUNKS
    loads = []
    for g in range(CHUNKS):
        for top in range(2):
            rows = pl.ds(top * half + g * step, step)
            load = pltpu.make_async_copy(x_hbm.at[rows], x_v.at[rows], load_sem.at[2 * g + top])
            load.start()
            loads.append(load)

    barrier = pltpu.get_barrier_semaphore()
    for k in range(1, rows_all):
        pl.semaphore_signal(barrier, inc=1, device_id=(other_row(k), col), device_id_type=MESH)
    for k in range(1, nx):
        for there in (row, beside):
            pl.semaphore_signal(barrier, inc=1, device_id=(there, other_col(k)), device_id_type=MESH)

    small[0].wait()
    for h in range(2):
        sloc[h] = smp_ref[:, h * 128 : (h + 1) * 128] & 127
    sidx[z, pl.ds(2 * y + c, 1), :] = sloc[c]
    small[1].wait()

    lane = lax.broadcasted_iota(jnp.int32, (128, 128), 1)
    eye = (lane == lax.broadcasted_iota(jnp.int32, (128, 128), 0)).astype(F32)
    flip = (1 - 2 * c).astype(F32)
    t_copies = []
    for g in range(CHUNKS):
        loads[2 * g].wait()
        loads[2 * g + 1].wait()

        def first(i, _):
            a = g * step + i
            d0 = (eye * sgn_ref[pl.ds(a, 1), :].astype(F32)).astype(BF16)
            d1 = (eye * (sgn_ref[pl.ds(half + a, 1), :].astype(F32) * flip)).astype(BF16)
            v0 = jnp.dot(d0, x_v[a], preferred_element_type=F32)
            v1 = jnp.dot(d1, x_v[half + a], preferred_element_type=F32)
            out_t[a] = v0 - v1
            own[a] = v0 + v1
            return 0

        lax.fori_loop(0, step, first, 0, unroll=4)
        if g == 0:
            pl.semaphore_wait(barrier, rows_all - 1 + 2 * (nx - 1))
        rows = pl.ds(g * step, step)
        copy = pltpu.make_async_remote_copy(
            src_ref=out_t.at[rows],
            dst_ref=in_t.at[rows],
            send_sem=t_send.at[g],
            recv_sem=t_recv.at[g],
            device_id=sibling,
            device_id_type=MESH,
        )
        copy.start()
        t_copies.append(copy)
        if g == 0:
            to_rows = []
            for k in range(1, rows_all):
                copy = pltpu.make_async_remote_copy(
                    src_ref=sloc.at[lax.rem(row + k, 2)],
                    dst_ref=sidx.at[z, pl.ds(2 * y + c, 1), :],
                    send_sem=i_send.at[k - 1],
                    recv_sem=i_recv.at[k - 1],
                    device_id=(other_row(k), col),
                    device_id_type=MESH,
                )
                copy.start()
                to_rows.append(copy)
            sent += to_rows
    sent += t_copies

    def transform(ref):
        def body(i, _):
            rows = pl.ds(pl.multiple_of(i * 8, 8), 8)
            v = [ref[a, rows, :] for a in range(half)]
            place = 1
            while place < half:
                for a in range(half):
                    if not a & place:
                        v[a], v[a | place] = v[a] + v[a | place], v[a] - v[a | place]
                place *= 2
            for a in range(half):
                ref[a, rows, :] = v[a]
            return 0

        lax.fori_loop(0, 16, body, 0)

    transform(own)

    for copy in to_rows:
        copy.wait_recv()
    nb = rows_all
    index = sidx[...].reshape(nb, 128).astype(F32)
    if nb < 128:
        index = jnp.concatenate([index, jnp.zeros((128 - nb, 128), F32)], axis=0)
    negative = lax.population_count(lane & row) & 1
    table[...] = (index.T.astype(jnp.int32) + 128 * negative).reshape(PAIRS, 8, 128)

    for copy in t_copies:
        copy.wait_recv()
    transform(in_t)

    lower = lax.broadcasted_iota(jnp.int32, (chips * 16, 128), 0) % 8 < 4
    place8 = lax.broadcasted_iota(jnp.int32, (8, 128), 1) + 128
    axes = {"z": (z, NZ, at_z), "y": (y, NY, at_y)}
    stages = {}
    firsts = [sum(kind[1] for kind in PARTS[:number]) for number in range(len(PARTS))]
    for number, (axis, pairs, longer, direct) in enumerate(PARTS):
        q, r1, f, r2, s1, v1, s2, v2 = part_refs[8 * number : 8 * number + 8]
        first_pair = firsts[number]
        n1, n2 = (NZ, NY) if axis == "z" else (NY, NZ)

        def one(p, i, signs):
            index = table[p]
            for place in range(chips):
                bz, by = (place // NY, place % NY) if axis == "z" else (place % NZ, place // NZ)
                rows = []
                for bc in range(2):
                    b = (bz * NY + by) * 2 + bc
                    ours = jnp.broadcast_to(index[:, b : b + 1], (8, 128)) & place8
                    rows.append((1 - 2 * (lax.population_count(ours) & 1)).astype(F32))
                here = pl.ds(place * 16, 16)
                signs[here, :128] = jnp.concatenate(rows, axis=0).astype(BF16)
                signs[here, 128:] = jnp.concatenate([rows[0], -rows[1]], axis=0).astype(BF16)
            field = jnp.concatenate(
                [
                    jnp.concatenate([own[2 * p], own[2 * p + 1]], axis=1),
                    jnp.concatenate([in_t[2 * p], in_t[2 * p + 1]], axis=1),
                ],
                axis=0,
            )
            high, low = split(field)
            both = jnp.dot(signs[...], high, preferred_element_type=F32) + jnp.dot(
                signs[...], low, preferred_element_type=F32
            )
            value = jnp.where(lower, both[:, :128], both[:, 128:])
            q[:, :, i] = value.reshape(n1, n2, 2, 8, 128)

        def product(i, _):
            one(first_pair + 2 * i, 2 * i, signs0)
            one(first_pair + 2 * i + 1, 2 * i + 1, signs1)
            return 0

        if pairs > 1:
            lax.fori_loop(0, pairs // 2, product, 0)
        if pairs % 2:
            one(first_pair + pairs - 1, pairs - 1, signs0)
        me, n, device = axes[axis]
        stages[number, 1] = Stage(me, n, longer, False, q, r1, s1, v1, device, sent)

    scale = float(8192 * nb) ** (-0.5)
    x_copies = []

    def finish(number):
        here = pl.ds(firsts[number], PARTS[number][1])
        sk[:, here] = jnp.swapaxes(stages[number, 2].total() * scale, 0, 1)
        for k in range(nx):
            for slot, there in enumerate((row, beside)):
                if k or slot:
                    copy = pltpu.make_async_remote_copy(
                        src_ref=sk.at[:, here],
                        dst_ref=xg.at[k, slot, :, here],
                        send_sem=x_send.at[k, slot, number],
                        recv_sem=x_recv.at[k, slot, number],
                        device_id=(there, other_col(k)),
                        device_id_type=MESH,
                    )
                    copy.start()
                    x_copies.append((number, copy))
                    sent.append(copy)

    gr = nx * 128 // nb
    per_x = chips // nx
    dims = (((0,), (0,)), ((), ()))

    def rows_of(ref, numbers):
        pieces = []
        for number in numbers:
            pieces.append(ref[:, firsts[number] : firsts[number] + PARTS[number][1]].reshape(-1, 128))
        return pieces

    def gram(numbers, begin):
        for number, copy in x_copies:
            if number in numbers:
                copy.wait_recv()
        near = split(jnp.concatenate(rows_of(sk, numbers) + rows_of(xg.at[0, 1], numbers), axis=0))
        for k in range(nx):
            if k:
                far = split(jnp.concatenate(rows_of(xg.at[k, 0], numbers) + rows_of(xg.at[k, 1], numbers), axis=0))
            else:
                far = near
            block = (
                lax.dot_general(far[0], near[0], dims, preferred_element_type=F32)
                + lax.dot_general(far[0], near[1], dims, preferred_element_type=F32)
                + lax.dot_general(far[1], near[0], dims, preferred_element_type=F32)
            ).reshape(per_x, 2, gr, 128)
            here = pl.ds(lax.rem(col + nx - k, nx) * per_x, per_x)
            for core in range(2):
                value = block[:, core]
                gbuf[core, here] = value if begin else gbuf[core, here] + value

    done = []
    for number, phase, direction, step in ORDER:
        if not stages[number, phase].take(direction, step):
            continue
        if phase == 2:
            finish(number)
            done.append(number)
            continue
        axis, pairs, longer, direct = PARTS[number]
        q, r1, f, r2, s1, v1, s2, v2 = part_refs[8 * number : 8 * number + 8]
        f[...] = stages[number, 1].total()
        me, n, device = axes["y" if axis == "z" else "z"]
        stages[number, 2] = Stage(me, n, longer, direct, f, r2, s2, v2, device, sent)
    gram(done[: len(done) // 2], True)
    gram(done[len(done) // 2 :], False)

    blocks = []
    for k in range(1, chips):
        there = other_chip(k)
        copy = pltpu.make_async_remote_copy(
            src_ref=gbuf.at[c, there],
            dst_ref=g2.at[k - 1],
            send_sem=h_send.at[k - 1],
            recv_sem=h_recv.at[k - 1],
            device_id=at_chip(there),
            device_id_type=MESH,
        )
        copy.start()
        blocks.append(copy)
    sk_out[c] = sk[c]
    sk_out[other] = xg[0, 1, c]
    for copy in sent:
        copy.wait_send()
    total = gbuf[c, chip]
    for k, copy in enumerate(blocks):
        copy.wait_recv()
        total = total + g2[k]
    g_out[...] = total * (1.0 / float(256 * nb))
    for copy in blocks:
        copy.wait_send()


def on_device(nx, design, row_signs, sampled):
    vm, dma = pltpu.VMEM, pltpu.SemaphoreType.DMA
    half = PAIRS * 2
    chips = NZ * NY
    gr = nx * 128 // (2 * chips)
    scratch = [
        vm((2 * half, 128, 128), BF16),
        vm((2 * half, 128), jnp.int32),
        vm((1, 256), jnp.int32),
        vm((half, 128, 128), F32),
        vm((half, 128, 128), F32),
        vm((half, 128, 128), F32),
        vm((2, 1, 128), jnp.int32),
        vm((NZ, 2 * NY, 128), jnp.int32),
        vm((PAIRS, 8, 128), jnp.int32),
        vm((chips * 16, 256), BF16),
        vm((chips * 16, 256), BF16),
        vm((2, PAIRS, 8, 128), F32),
        vm((nx, 2, 2, PAIRS, 8, 128), F32),
        vm((2, chips, gr, 128), F32),
        vm((chips - 1, gr, 128), F32),
        dma((2 * CHUNKS + 2,)),
        dma((CHUNKS,)),
        dma((CHUNKS,)),
        dma((2 * chips - 1,)),
        dma((2 * chips - 1,)),
        dma((nx, 2, len(PARTS))),
        dma((nx, 2, len(PARTS))),
        dma((chips - 1,)),
        dma((chips - 1,)),
    ]
    for axis, pairs, _, _ in PARTS:
        n1, n2 = (NZ, NY) if axis == "z" else (NY, NZ)
        scratch += [
            vm((n1, n2, pairs, 2, 8, 128), F32),
            vm((n1 - 1, n2, pairs, 2, 8, 128), F32),
            vm((n2, pairs, 2, 8, 128), F32),
            vm((n2 - 1, pairs, 2, 8, 128), F32),
            dma((n1 - 1,)),
            dma((n1 - 1,)),
            dma((n2 - 1,)),
            dma((n2 - 1,)),
        ]
    sketch, gram = pl.pallas_call(
        functools.partial(kernel, nx),
        out_shape=(
            jax.ShapeDtypeStruct((2, PAIRS, 8, 128), F32),
            jax.ShapeDtypeStruct((gr, 128), F32),
        ),
        in_specs=[
            pl.BlockSpec(memory_space=pltpu.HBM),
            pl.BlockSpec(memory_space=pltpu.HBM),
            pl.BlockSpec(memory_space=pltpu.HBM),
        ],
        out_specs=(pl.BlockSpec(memory_space=pltpu.VMEM), pl.BlockSpec(memory_space=pltpu.VMEM)),
        scratch_shapes=scratch,
        compiler_params=pltpu.CompilerParams(
            collective_id=0, has_side_effects=True, vmem_limit_bytes=62 * 1024 * 1024
        ),
    )(design.reshape(2 * half, 128, 128), row_signs.reshape(2 * half, 128), sampled)
    return sketch.reshape(256, 128), gram


def solution(mesh):
    return jax.shard_map(
        functools.partial(on_device, mesh.shape["col"]),
        mesh=mesh,
        in_specs=(P("row", "col"), P("row"), P("row", None)),
        out_specs=(P("row", "col"), P("row", "col")),
        check_vma=False,
    )
```

time: 919 us -> 71.6 us (0.08)
  waiting for transfers between devices: 820 us -> 0 us
  Pallas kernels: 0 us -> 68 us
  other arithmetic: 40.4 us -> 0 us
  matrix products: 16.9 us -> 0 us
  between operations: 14.7 us -> 0.64 us
  starting transfers between devices: 10.9 us -> 0 us
  blocking collectives: 10.6 us -> 0 us
    ppermute x6 -> x0, waiting for transfers between devices: 644 us -> none  [partner_2(): lax.ppermute(value, axis, [(i, i ^ 1 << stride) for i in range(lax.axis_s...]
    unnamed x2 -> x0, waiting for transfers between devices: 176 us -> none
    pallas_call x0 -> x1, Pallas kernels: none -> 68 us  [on_device(): pl.pallas_call(functools.partial(kernel, nx), out_shape=(jax.ShapeDtypeSt...]
    select_n x7 -> x0, other arithmetic: 35.1 us -> none  [the longest x6 35.1 us: on_device(): field = jnp.where(is_upper, partner - field, field + partner)]
    dot_general x3 -> x0, matrix products: 16.9 us -> none  [the longest x1 8.96 us: on_device(): jnp.einsum('ij,ajc->aic', hadamard(128), field, precision=lax.Precision.H...]
    ppermute x6 -> x0, starting transfers between devices: 10.9 us -> none  [partner_2(): lax.ppermute(value, axis, [(i, i ^ 1 << stride) for i in range(lax.axis_s...]
    all_gather x1 -> x0, blocking collectives: 10.6 us -> none  [on_device(): all_columns = lax.all_gather(picked, 'col', axis=1, tiled=True)]
  transfers between devices with their start and end apart: 7 -> 0, of which waited for: 7 -> 0; matrix products, arithmetic and copies ran while one was open for 0% -> 0% of each run, Pallas kernels for 0% -> 0%
where the time goes in v2:
time: 71.6 us; the launch traced here: 71.5 us
  Pallas kernels  68 us (95%)
  local copies, waits for them, and re-layouts  2.85 us (4%)
    pallas_call x1, Pallas kernels, on_device(): pl.pallas_call(functools.partial(kernel, nx), out_shape=(jax.ShapeDtypeSt...  68 us
    unnamed x2, local copies, waits for them, and re-layouts  2.85 us

profile of v2, /device:TPU:1, one launch (start us, length us, event | category | flops | bytes accessed | tf_op | source)
XLA Modules:
  0.0 71.5 jit_solution(10688954197772772265)
XLA Ops:
  0.6 68.0 %shard_map.50 = (f32[2,16,8,128]{3,2,1,0:T(8,128)}, f32[8,128]{1,0:T(8,128)}) custom-call(bf16[64,128,128]{2,1,0:T(8,128)(2,1)} %bitcast.3, s32[64,128]{1,0:T(8,128)} %bitcast.5, s32[1,256]{1,0:T(1,128)} %smp_hbm.1), custom_call_target="tpu_custom_call" | custom-call | tf_op jit(solution)/shard_map/pallas_call | solution.py:456
  68.6 1.6 %copy.7 = f32[256,128]{1,0:T(8,128)} copy(f32[256,128]{1,0:T(8,128)} %bitcast.4) | data formatting | bytes 262144
  70.2 1.3 %copy.8 = f32[8,128]{1,0:T(8,128)} copy(f32[8,128]{1,0:T(8,128)} %get-tuple-element.9) | data formatting | bytes 8192

commit v3 on v2

--- a/solution.py
+++ b/solution.py
@@ -12,26 +12,25 @@
 F32, BF16 = jnp.float32, jnp.bfloat16
 CHUNKS = 4
 PAIRS = 16
+LATE = 2
 PARTS = (
-    ("z", 2, 0, True),
-    ("y", 2, 0, False),
-    ("z", 2, 1, True),
-    ("y", 2, 1, False),
-    ("z", 2, 0, True),
-    ("y", 2, 0, False),
-    ("z", 2, 1, True),
-    ("y", 2, 1, False),
+    ("z", 2, 1, 1),
+    ("y", 2, 0, 2),
+    ("z", 2, 0, 1),
+    ("y", 2, 1, 2),
+    ("z", 2, 0, 1),
+    ("z", 2, 1, 1),
+    ("y", 2, 0, 2),
+    ("y", 2, 1, 2),
 )
 ORDER = (
     (0, 1, 0, 1), (0, 1, 1, 1), (2, 1, 0, 1), (2, 1, 1, 1), (1, 1, 0, 1), (1, 1, 1, 1), (4, 1, 0, 1), (4, 1, 1, 1),
-    (0, 1, 0, 2), (3, 1, 0, 1), (3, 1, 1, 1), (0, 1, 1, 2), (6, 1, 0, 1), (6, 1, 1, 1), (2, 1, 0, 2), (5, 1, 0, 1),
-    (5, 1, 1, 1), (2, 1, 1, 2), (4, 1, 0, 2), (4, 1, 1, 2), (0, 1, 0, 3), (7, 1, 0, 1), (7, 1, 1, 1), (0, 1, 1, 3),
-    (6, 1, 0, 2), (6, 1, 1, 2), (2, 1, 0, 3), (1, 1, 0, 2), (3, 1, 1, 2), (2, 1, 1, 3), (4, 1, 0, 3), (4, 1, 1, 3),
-    (0, 1, 0, 4), (5, 1, 0, 2), (7, 1, 1, 2), (6, 1, 1, 3), (1, 2, 1, 1), (3, 2, 1, 1), (6, 1, 0, 3), (1, 2, 0, 1),
-    (3, 2, 0, 1), (2, 1, 1, 4), (5, 2, 1, 1), (7, 2, 1, 1), (4, 1, 0, 4), (5, 2, 0, 1), (0, 2, 0, 1), (7, 2, 0, 1),
-    (1, 2, 0, 2), (6, 1, 1, 4), (3, 2, 0, 2), (1, 2, 1, 2), (3, 2, 1, 2), (5, 2, 1, 2), (2, 2, 0, 1), (7, 2, 1, 2),
-    (5, 2, 0, 2), (7, 2, 0, 2), (4, 2, 0, 1), (1, 2, 0, 3), (3, 2, 0, 3), (1, 2, 1, 3), (3, 2, 1, 3), (6, 2, 0, 1),
-    (5, 2, 1, 3), (7, 2, 1, 3), (5, 2, 0, 3), (7, 2, 0, 3), (1, 2, 0, 4), (3, 2, 1, 4), (7, 2, 1, 4), (5, 2, 0, 4),
+    (5, 1, 0, 1), (5, 1, 1, 1), (3, 1, 0, 1), (3, 1, 1, 1), (0, 1, 0, 2), (0, 1, 1, 2), (2, 1, 0, 2), (2, 1, 1, 2),
+    (6, 1, 0, 1), (6, 1, 1, 1), (4, 1, 0, 2), (4, 1, 1, 2), (5, 1, 0, 2), (5, 1, 1, 2), (7, 1, 0, 1), (7, 1, 1, 1),
+    (0, 1, 0, 3), (0, 1, 1, 3), (2, 1, 0, 3), (2, 1, 1, 3), (1, 1, 0, 2), (3, 1, 1, 2), (4, 1, 0, 3), (4, 1, 1, 3),
+    (5, 1, 0, 3), (5, 1, 1, 3), (6, 1, 0, 2), (7, 1, 1, 2), (0, 1, 1, 4), (2, 1, 0, 4), (1, 2, 0, 1), (3, 2, 0, 1),
+    (5, 1, 1, 4), (4, 1, 0, 4), (0, 2, 0, 1), (2, 2, 0, 1), (6, 2, 0, 1), (7, 2, 0, 1), (1, 2, 0, 2), (3, 2, 0, 2),
+    (5, 2, 0, 1), (4, 2, 0, 1), (6, 2, 0, 2), (7, 2, 0, 2),
 )
 
 
@@ -41,75 +40,86 @@
 
 
 class Arm:
-    def __init__(self, me, n, step, reach, own, recv, slot, send_sem, recv_sem, device, sent):
-        self.me, self.n, self.step, self.reach, self.own = me, n, step, reach, own
-        self.recv, self.slot, self.sent = recv, slot, sent
-        self.send_sem, self.recv_sem = send_sem, recv_sem
-        self.device = device(self.at(step))
+    def __init__(self, stage, step, reach, slot):
+        self.stage, self.step, self.reach, self.slot = stage, step, reach, slot
         self.copies = {}
-
-    def at(self, offset):
-        return lax.rem(self.me + self.n + offset, self.n)
 
     def start(self, s):
         if not 1 <= s <= self.reach:
             return
-        index = self.slot + s - 1
-        source = self.own(self.at(self.step * self.reach)) if s == 1 else self.recv.at[index - 1]
+        stage, index = self.stage, self.slot + s - 1
+        source = stage.source.at[stage.at(self.step * self.reach)] if s == 1 else stage.recv.at[index - 1]
+        self.copies[s] = stage.send(index, source, self.step)
+
+    def take(self, s):
+        self.copies[s].wait_recv()
+        if s < self.reach:
+            stage = self.stage
+            here = stage.recv.at[self.slot + s - 1]
+            here[...] = here[...] + stage.source[stage.at(self.step * (self.reach - s))]
+            self.start(s + 1)
+
+
+class Stage:
+    def __init__(self, me, n, longer, scheme, source, recv, send_sem, recv_sem, device, sent):
+        self.me, self.n, self.source, self.recv = me, n, source, recv
+        self.send_sem, self.recv_sem, self.device, self.sent = send_sem, recv_sem, device, sent
+        self.arms = []
+        self.two = scheme == 2 and n == 8
+        self.direct = scheme > 0 and not self.two
+        if self.two:
+            s = self.side = -1 if longer else 1
+            self.copies = [
+                self.send(0, source.at[self.at(-s)], -s),
+                self.send(1, source.at[self.at(s)], s),
+                self.send(2, source.at[self.at(-3 * s)], -s),
+                self.send(3, source.at[self.at(-4 * s)], -2 * s),
+                self.send(4, source.at[self.at(3 * s)], s),
+            ]
+            self.left, self.last = 2, [0, 1, 5, 6]
+        elif self.direct:
+            self.copies = [self.send(k - 1, source.at[self.at(k)], k) for k in range(1, n)]
+            self.left, self.last = 1, list(range(n - 1))
+        else:
+            long, short = n // 2, n - 1 - n // 2
+            up, down = (short, long) if longer else (long, short)
+            for step, reach, slot in ((1, up, 0), (-1, down, up)):
+                self.arms.append(Arm(self, step, reach, slot))
+                self.arms[-1].start(1)
+            self.left = n - 1
+            self.last = [arm.slot + arm.reach - 1 for arm in self.arms if arm.reach]
+
+    def at(self, offset):
+        return lax.rem(self.me + self.n + offset, self.n)
+
+    def send(self, slot, source, offset):
         copy = pltpu.make_async_remote_copy(
             src_ref=source,
-            dst_ref=self.recv.at[index],
-            send_sem=self.send_sem.at[index],
-            recv_sem=self.recv_sem.at[index],
-            device_id=self.device,
+            dst_ref=self.recv.at[slot],
+            send_sem=self.send_sem.at[slot],
+            recv_sem=self.recv_sem.at[slot],
+            device_id=self.device(self.at(offset)),
             device_id_type=MESH,
         )
         copy.start()
-        self.copies[s] = copy
         self.sent.append(copy)
-
-    def take(self, s):
-        self.copies[s].wait_recv()
-        if s < self.reach:
-            here = self.recv.at[self.slot + s - 1]
-            here[...] = here[...] + self.own(self.at(self.step * (self.reach - s)))[...]
-            self.start(s + 1)
-
-
-class Stage:
-    def __init__(self, me, n, longer, direct, source, recv, send_sem, recv_sem, device, sent):
-        self.me, self.source, self.recv = me, source, recv
-        self.direct = []
-        self.arms = []
-        if direct:
-            for k in range(1, n):
-                there = lax.rem(me + k, n)
-                copy = pltpu.make_async_remote_copy(
-                    src_ref=source.at[there],
-                    dst_ref=recv.at[k - 1],
-                    send_sem=send_sem.at[k - 1],
-                    recv_sem=recv_sem.at[k - 1],
-                    device_id=device(there),
-                    device_id_type=MESH,
-                )
-                copy.start()
-                sent.append(copy)
-                self.direct.append(copy)
-            self.left = 1
-            self.last = list(range(n - 1))
-            return
-        long, short = n // 2, n - 1 - n // 2
-        up, down = (short, long) if longer else (long, short)
-        own = lambda t: source.at[t]
-        for step, reach, slot in ((1, up, 0), (-1, down, up)):
-            self.arms.append(Arm(me, n, step, reach, own, recv, slot, send_sem, recv_sem, device, sent))
-            self.arms[-1].start(1)
-        self.left = n - 1
-        self.last = [arm.slot + arm.reach - 1 for arm in self.arms if arm.reach]
+        return copy
 
     def take(self, direction, step):
-        if self.direct:
-            for copy in self.direct:
+        if self.two and step == 1:
+            for slot in (2, 3, 4):
+                self.copies[slot].wait_recv()
+            s = self.side
+            self.recv[2] = self.recv[2] + self.recv[3] + self.source[self.at(-2 * s)]
+            self.recv[4] = self.recv[4] + self.source[self.at(2 * s)]
+            self.copies += [self.send(5, self.recv.at[2], -2 * s), self.send(6, self.recv.at[4], 2 * s)]
+        elif self.two:
+            for slot in self.last:
+                self.copies[slot].wait_recv()
+        elif self.direct:
+            if step > 1:
+                return False
+            for copy in self.copies:
                 copy.wait_recv()
         elif step <= self.arms[direction].reach:
             self.arms[direction].take(step)
@@ -127,7 +137,7 @@
 
 def kernel(
     nx, x_hbm, sgn_hbm, smp_hbm, sk_out, g_out,
-    x_v, sgn_ref, smp_ref, own, out_t, in_t, sloc, sidx, table, signs0, signs1, sk, xg, gbuf, g2,
+    x_v, sgn_ref, smp_ref, own, out_t, in_t, sloc, sidx, table, signs0, signs1, sk, beside_sk, packed, xg, gbuf, g2,
     load_sem, t_send, t_recv, i_send, i_recv, x_send, x_recv, h_send, h_recv, *part_refs,
 ):
     row, col = lax.axis_index("row"), lax.axis_index("col")
@@ -187,7 +197,6 @@
     small[0].wait()
     for h in range(2):
         sloc[h] = smp_ref[:, h * 128 : (h + 1) * 128] & 127
-    sidx[z, pl.ds(2 * y + c, 1), :] = sloc[c]
     small[1].wait()
 
     lane = lax.broadcasted_iota(jnp.int32, (128, 128), 1)
@@ -223,19 +232,18 @@
         copy.start()
         t_copies.append(copy)
         if g == 0:
-            to_rows = []
+            pltpu.make_async_copy(sloc.at[c], sidx.at[pl.ds(row, 1)], i_recv.at[0]).start()
             for k in range(1, rows_all):
                 copy = pltpu.make_async_remote_copy(
                     src_ref=sloc.at[lax.rem(row + k, 2)],
-                    dst_ref=sidx.at[z, pl.ds(2 * y + c, 1), :],
+                    dst_ref=sidx.at[pl.ds(row, 1)],
                     send_sem=i_send.at[k - 1],
-                    recv_sem=i_recv.at[k - 1],
+                    recv_sem=i_recv.at[0],
                     device_id=(other_row(k), col),
                     device_id_type=MESH,
                 )
                 copy.start()
-                to_rows.append(copy)
-            sent += to_rows
+                sent.append(copy)
     sent += t_copies
 
     def transform(ref):
@@ -256,10 +264,9 @@
 
     transform(own)
 
-    for copy in to_rows:
-        copy.wait_recv()
+    pltpu.make_async_copy(sidx, sidx, i_recv.at[0]).wait()
     nb = rows_all
-    index = sidx[...].reshape(nb, 128).astype(F32)
+    index = sidx[...].astype(F32)
     if nb < 128:
         index = jnp.concatenate([index, jnp.zeros((128 - nb, 128), F32)], axis=0)
     negative = lax.population_count(lane & row) & 1
@@ -315,7 +322,7 @@
         if pairs % 2:
             one(first_pair + pairs - 1, pairs - 1, signs0)
         me, n, device = axes[axis]
-        stages[number, 1] = Stage(me, n, longer, False, q, r1, s1, v1, device, sent)
+        stages[number, 1] = Stage(me, n, longer, 0, q, r1, s1, v1, device, sent)
 
     scale = float(8192 * nb) ** (-0.5)
     x_copies = []
@@ -323,50 +330,71 @@
     def finish(number):
         here = pl.ds(firsts[number], PARTS[number][1])
         sk[:, here] = jnp.swapaxes(stages[number, 2].total() * scale, 0, 1)
-        for k in range(nx):
-            for slot, there in enumerate((row, beside)):
-                if k or slot:
-                    copy = pltpu.make_async_remote_copy(
-                        src_ref=sk.at[:, here],
-                        dst_ref=xg.at[k, slot, :, here],
-                        send_sem=x_send.at[k, slot, number],
-                        recv_sem=x_recv.at[k, slot, number],
-                        device_id=(there, other_col(k)),
-                        device_id_type=MESH,
-                    )
-                    copy.start()
-                    x_copies.append((number, copy))
-                    sent.append(copy)
+        value = sk[:, here]
+        for h in range(2):
+            lanes = slice(64 * h, 64 * h + 64)
+            packed[h, here] = jnp.concatenate([value[0, :, :, lanes], value[1, :, :, lanes]], axis=2)
+
+        def send(slot, source, target, device):
+            copy = pltpu.make_async_remote_copy(
+                src_ref=source,
+                dst_ref=target,
+                send_sem=x_send.at[slot, number],
+                recv_sem=x_recv.at[slot, number],
+                device_id=device,
+                device_id_type=MESH,
+            )
+            copy.start()
+            x_copies.append((number, copy))
+            sent.append(copy)
+
+        send(0, sk.at[:, here], beside_sk.at[:, here], sibling)
+        for k in range(1, nx):
+            send(2 * k - 1, packed.at[c, here], xg.at[k, 0, here], (row, other_col(k)))
+            send(2 * k, packed.at[other, here], xg.at[k, 1, here], (beside, other_col(k)))
 
     gr = nx * 128 // nb
-    per_x = chips // nx
+    per_x = rows_all // nx
+    group = per_x // 2
     dims = (((0,), (0,)), ((), ()))
 
-    def rows_of(ref, numbers):
-        pieces = []
-        for number in numbers:
-            pieces.append(ref[:, firsts[number] : firsts[number] + PARTS[number][1]].reshape(-1, 128))
-        return pieces
+    def rows_of(get, numbers):
+        return jnp.concatenate(
+            [get(pl.ds(firsts[number], PARTS[number][1])).reshape(-1, 128) for number in numbers], axis=0
+        )
 
     def gram(numbers, begin):
         for number, copy in x_copies:
             if number in numbers:
                 copy.wait_recv()
-        near = split(jnp.concatenate(rows_of(sk, numbers) + rows_of(xg.at[0, 1], numbers), axis=0))
+        near, far = [], []
+        for core, ref in enumerate((sk, beside_sk)):
+            near.append(
+                jnp.concatenate([rows_of(lambda here, bc=bc: ref[bc, here], numbers) for bc in range(2)], axis=1)
+            )
+        near = split(jnp.concatenate(near, axis=0))
         for k in range(nx):
             if k:
-                far = split(jnp.concatenate(rows_of(xg.at[k, 0], numbers) + rows_of(xg.at[k, 1], numbers), axis=0))
+                far = [rows_of(lambda here, core=core: xg[k, core, here], numbers) for core in range(2)]
             else:
-                far = near
-            block = (
+                far = [rows_of(lambda here: packed[c, here], numbers)]
+                halves = [
+                    jnp.concatenate(
+                        [rows_of(lambda here, bc=bc: beside_sk[bc, here], numbers)[:, 64 * h : 64 * h + 64] for bc in range(2)],
+                        axis=1,
+                    )
+                    for h in range(2)
+                ]
+                far.append(jnp.where(c == 0, halves[0], halves[1]))
+            far = split(jnp.concatenate(far, axis=0))
+            both = (
                 lax.dot_general(far[0], near[0], dims, preferred_element_type=F32)
                 + lax.dot_general(far[0], near[1], dims, preferred_element_type=F32)
                 + lax.dot_general(far[1], near[0], dims, preferred_element_type=F32)
-            ).reshape(per_x, 2, gr, 128)
-            here = pl.ds(lax.rem(col + nx - k, nx) * per_x, per_x)
-            for core in range(2):
-                value = block[:, core]
-                gbuf[core, here] = value if begin else gbuf[core, here] + value
+            )
+            block = (both[:64, :128] + both[64:, 128:]).reshape(group, gr, 128)
+            here = pl.ds(lax.rem(col + nx - k, nx) * group, group)
+            gbuf[here] = block if begin else gbuf[here] + block
 
     done = []
     for number, phase, direction, step in ORDER:
@@ -381,33 +409,41 @@
         f[...] = stages[number, 1].total()
         me, n, device = axes["y" if axis == "z" else "z"]
         stages[number, 2] = Stage(me, n, longer, direct, f, r2, s2, v2, device, sent)
-    gram(done[: len(done) // 2], True)
-    gram(done[len(done) // 2 :], False)
-
-    blocks = []
-    for k in range(1, chips):
-        there = other_chip(k)
-        copy = pltpu.make_async_remote_copy(
-            src_ref=gbuf.at[c, there],
-            dst_ref=g2.at[k - 1],
-            send_sem=h_send.at[k - 1],
-            recv_sem=h_recv.at[k - 1],
-            device_id=at_chip(there),
+    gram(done[:-LATE], True)
+    gram(done[-LATE:], False)
+
+    in_half = lax.rem(row, per_x)
+    first_block = row // per_x * group + lax.rem(in_half, group)
+    here_too = in_half // group == c
+
+    def to_target(k):
+        t = lax.rem(first_block + k, chips)
+        return pltpu.make_async_remote_copy(
+            src_ref=gbuf.at[t],
+            dst_ref=g2.at[chip],
+            send_sem=h_send.at[k],
+            recv_sem=h_recv.at[0],
+            device_id=(t // group * per_x + c * group + lax.rem(t, group), col),
             device_id_type=MESH,
         )
+
+    blocks = [to_target(k) for k in range(chips)]
+    for copy in blocks[1:]:
         copy.start()
-        blocks.append(copy)
+    pl.when(jnp.logical_not(here_too))(blocks[0].start)
+
+    own_block = pltpu.make_async_copy(gbuf.at[first_block], g2.at[chip], h_recv.at[0])
+    pl.when(here_too)(own_block.start)
+
     sk_out[c] = sk[c]
-    sk_out[other] = xg[0, 1, c]
+    sk_out[other] = beside_sk[c]
     for copy in sent:
         copy.wait_send()
-    total = gbuf[c, chip]
-    for k, copy in enumerate(blocks):
-        copy.wait_recv()
-        total = total + g2[k]
-    g_out[...] = total * (1.0 / float(256 * nb))
-    for copy in blocks:
+    for copy in blocks[1:]:
         copy.wait_send()
+    pl.when(jnp.logical_not(here_too))(blocks[0].wait_send)
+    pltpu.make_async_copy(g2, g2, h_recv.at[0]).wait()
+    g_out[...] = jnp.sum(g2[...], axis=0) * (1.0 / float(256 * nb))
 
 
 def on_device(nx, design, row_signs, sampled):
@@ -423,23 +459,25 @@
         vm((half, 128, 128), F32),
         vm((half, 128, 128), F32),
         vm((2, 1, 128), jnp.int32),
-        vm((NZ, 2 * NY, 128), jnp.int32),
+        vm((2 * chips, 128), jnp.int32),
         vm((PAIRS, 8, 128), jnp.int32),
         vm((chips * 16, 256), BF16),
         vm((chips * 16, 256), BF16),
         vm((2, PAIRS, 8, 128), F32),
-        vm((nx, 2, 2, PAIRS, 8, 128), F32),
-        vm((2, chips, gr, 128), F32),
-        vm((chips - 1, gr, 128), F32),
+        vm((2, PAIRS, 8, 128), F32),
+        vm((2, PAIRS, 8, 128), F32),
+        vm((nx, 2, PAIRS, 8, 128), F32),
+        vm((chips, gr, 128), F32),
+        vm((chips, gr, 128), F32),
         dma((2 * CHUNKS + 2,)),
         dma((CHUNKS,)),
         dma((CHUNKS,)),
         dma((2 * chips - 1,)),
-        dma((2 * chips - 1,)),
-        dma((nx, 2, len(PARTS))),
-        dma((nx, 2, len(PARTS))),
-        dma((chips - 1,)),
-        dma((chips - 1,)),
+        dma((1,)),
+        dma((2 * nx - 1, len(PARTS))),
+        dma((2 * nx - 1, len(PARTS))),
+        dma((chips,)),
+        dma((1,)),
     ]
     for axis, pairs, _, _ in PARTS:
         n1, n2 = (NZ, NY) if axis == "z" else (NY, NZ)
@@ -467,9 +505,14 @@
         out_specs=(pl.BlockSpec(memory_space=pltpu.VMEM), pl.BlockSpec(memory_space=pltpu.VMEM)),
         scratch_shapes=scratch,
         compiler_params=pltpu.CompilerParams(
-            collective_id=0, has_side_effects=True, vmem_limit_bytes=62 * 1024 * 1024
+            collective_id=0, has_side_effects=True, vmem_limit_bytes=48 * 1024 * 1024
         ),
-    )(design.reshape(2 * half, 128, 128), row_signs.reshape(2 * half, 128), sampled)
+    )(
+        *(
+            pltpu.with_memory_space_constraint(value, pltpu.HBM)
+            for value in (design.reshape(2 * half, 128, 128), row_signs.reshape(2 * half, 128), sampled)
+        )
+    )
     return sketch.reshape(256, 128), gram
 
 

time: 71.6 us -> 67 us (0.936)
  Pallas kernels: 68 us -> 65 us
  local copies, waits for them, and re-layouts: 2.85 us -> 1.25 us
    pallas_call x1, Pallas kernels: 68 us -> 65 us  [on_device(): pl.pallas_call(functools.partial(kernel, nx), out_shape=(jax.ShapeDtypeSt...]
    unnamed x2, local copies, waits for them, and re-layouts: 2.85 us -> 1.25 us
where the time goes in v3:
time: 67 us; the launch traced here: 66.9 us
  Pallas kernels  65 us (97%)
  local copies, waits for them, and re-layouts  1.25 us (2%)
    pallas_call x1, Pallas kernels, on_device(): pl.pallas_call(functools.partial(kernel, nx), out_shape=(jax.ShapeDtypeSt...  65 us

profile of v3, /device:TPU:1, one launch (start us, length us, event | category | flops | bytes accessed | tf_op | source)
XLA Modules:
  0.0 66.9 jit_solution(16916442402292047940)
XLA Ops:
  0.6 65.0 %shard_map.50 = (f32[2,16,8,128]{3,2,1,0:T(8,128)S(1)}, f32[8,128]{1,0:T(8,128)S(1)}) custom-call(bf16[64,128,128]{2,1,0:T(8,128)(2,1)} %bitcast.4, s32[64,128]{1,0:T(8,128)} %bitcast.5, s32[1,256]{1,0:T(1,128)} %smp_hbm.1), custom_call_target="tpu_custom_call" | custom-call | tf_op jit(solution)/shard_map/pallas_call | solution.py:494
  65.7 0.7 copy.7
  66.3 0.6 copy.8

commit v4 on v3

--- a/solution.py
+++ b/solution.py
@@ -39,6 +39,14 @@
     return high, (v - high.astype(F32)).astype(BF16)
 
 
+def arrived(ref, sem):
+    pltpu.make_async_copy(ref, ref, sem).wait()
+
+
+def far_first(n):
+    return sorted(range(1, n), key=lambda k: -min(k, n - k))
+
+
 class Arm:
     def __init__(self, stage, step, reach, slot):
         self.stage, self.step, self.reach, self.slot = stage, step, reach, slot
@@ -61,24 +69,23 @@
 
 
 class Stage:
-    def __init__(self, me, n, longer, scheme, source, recv, send_sem, recv_sem, device, sent):
+    def __init__(self, me, n, longer, scheme, source, recv, send_sem, recv_sem, device):
         self.me, self.n, self.source, self.recv = me, n, source, recv
-        self.send_sem, self.recv_sem, self.device, self.sent = send_sem, recv_sem, device, sent
+        self.send_sem, self.recv_sem, self.device = send_sem, recv_sem, device
         self.arms = []
         self.two = scheme == 2 and n == 8
         self.direct = scheme > 0 and not self.two
         if self.two:
             s = self.side = -1 if longer else 1
-            self.copies = [
-                self.send(0, source.at[self.at(-s)], -s),
-                self.send(1, source.at[self.at(s)], s),
-                self.send(2, source.at[self.at(-3 * s)], -s),
-                self.send(3, source.at[self.at(-4 * s)], -2 * s),
-                self.send(4, source.at[self.at(3 * s)], s),
-            ]
+            self.send(2, source.at[self.at(-3 * s)], -s)
+            self.send(3, source.at[self.at(-4 * s)], -2 * s)
+            self.send(4, source.at[self.at(3 * s)], s)
+            self.send(0, source.at[self.at(-s)], -s)
+            self.send(1, source.at[self.at(s)], s)
             self.left, self.last = 2, [0, 1, 5, 6]
         elif self.direct:
-            self.copies = [self.send(k - 1, source.at[self.at(k)], k) for k in range(1, n)]
+            for k in range(1, n):
+                self.send(k - 1, source.at[self.at(k)], k)
             self.left, self.last = 1, list(range(n - 1))
         else:
             long, short = n // 2, n - 1 - n // 2
@@ -93,34 +100,38 @@
         return lax.rem(self.me + self.n + offset, self.n)
 
     def send(self, slot, source, offset):
+        if self.two:
+            arrival = 0 if slot in (2, 3, 4) else 1
+        else:
+            arrival = 0 if self.direct else slot
         copy = pltpu.make_async_remote_copy(
             src_ref=source,
             dst_ref=self.recv.at[slot],
-            send_sem=self.send_sem.at[slot],
-            recv_sem=self.recv_sem.at[slot],
+            send_sem=self.send_sem.at[0],
+            recv_sem=self.recv_sem.at[arrival],
             device_id=self.device(self.at(offset)),
             device_id_type=MESH,
         )
         copy.start()
-        self.sent.append(copy)
         return copy
+
+    def wait_sends(self):
+        arrived(self.recv, self.send_sem.at[0])
 
     def take(self, direction, step):
         if self.two and step == 1:
-            for slot in (2, 3, 4):
-                self.copies[slot].wait_recv()
+            arrived(self.recv.at[pl.ds(2, 3)], self.recv_sem.at[0])
             s = self.side
             self.recv[2] = self.recv[2] + self.recv[3] + self.source[self.at(-2 * s)]
+            self.send(5, self.recv.at[2], -2 * s)
             self.recv[4] = self.recv[4] + self.source[self.at(2 * s)]
-            self.copies += [self.send(5, self.recv.at[2], -2 * s), self.send(6, self.recv.at[4], 2 * s)]
+            self.send(6, self.recv.at[4], 2 * s)
         elif self.two:
-            for slot in self.last:
-                self.copies[slot].wait_recv()
+            arrived(self.recv.at[pl.ds(0, 4)], self.recv_sem.at[1])
         elif self.direct:
             if step > 1:
                 return False
-            for copy in self.copies:
-                copy.wait_recv()
+            arrived(self.recv, self.recv_sem.at[0])
         elif step <= self.arms[direction].reach:
             self.arms[direction].take(step)
         else:
@@ -147,7 +158,6 @@
     z = chip // NY
     chips = NZ * NY
     half = PAIRS * 2
-    sent = []
 
     rows_all = 2 * chips
     other = 1 - c
@@ -175,20 +185,18 @@
 
     small = []
     for number, (source, target) in enumerate(((smp_hbm, smp_ref), (sgn_hbm, sgn_ref))):
-        load = pltpu.make_async_copy(source, target, load_sem.at[2 * CHUNKS + number])
+        load = pltpu.make_async_copy(source, target, load_sem.at[CHUNKS + number])
         load.start()
         small.append(load)
     step = half // CHUNKS
-    loads = []
     for g in range(CHUNKS):
         for top in range(2):
             rows = pl.ds(top * half + g * step, step)
-            load = pltpu.make_async_copy(x_hbm.at[rows], x_v.at[rows], load_sem.at[2 * g + top])
+            load = pltpu.make_async_copy(x_hbm.at[rows], x_v.at[rows], load_sem.at[g])
             load.start()
-            loads.append(load)
 
     barrier = pltpu.get_barrier_semaphore()
-    for k in range(1, rows_all):
+    for k in far_first(rows_all):
         pl.semaphore_signal(barrier, inc=1, device_id=(other_row(k), col), device_id_type=MESH)
     for k in range(1, nx):
         for there in (row, beside):
@@ -197,15 +205,25 @@
     small[0].wait()
     for h in range(2):
         sloc[h] = smp_ref[:, h * 128 : (h + 1) * 128] & 127
+    pl.semaphore_wait(barrier, rows_all - 1 + 2 * (nx - 1))
+    pltpu.make_async_copy(sloc.at[c], sidx.at[pl.ds(row, 1)], i_recv.at[0]).start()
+    for k in far_first(rows_all):
+        copy = pltpu.make_async_remote_copy(
+            src_ref=sloc.at[lax.rem(row + k, 2)],
+            dst_ref=sidx.at[pl.ds(row, 1)],
+            send_sem=i_send.at[0],
+            recv_sem=i_recv.at[0],
+            device_id=(other_row(k), col),
+            device_id_type=MESH,
+        )
+        copy.start()
     small[1].wait()
 
     lane = lax.broadcasted_iota(jnp.int32, (128, 128), 1)
     eye = (lane == lax.broadcasted_iota(jnp.int32, (128, 128), 0)).astype(F32)
     flip = (1 - 2 * c).astype(F32)
-    t_copies = []
     for g in range(CHUNKS):
-        loads[2 * g].wait()
-        loads[2 * g + 1].wait()
+        arrived(x_v.at[pl.ds(0, 2 * step)], load_sem.at[g])
 
         def first(i, _):
             a = g * step + i
@@ -218,33 +236,16 @@
             return 0
 
         lax.fori_loop(0, step, first, 0, unroll=4)
-        if g == 0:
-            pl.semaphore_wait(barrier, rows_all - 1 + 2 * (nx - 1))
         rows = pl.ds(g * step, step)
         copy = pltpu.make_async_remote_copy(
             src_ref=out_t.at[rows],
             dst_ref=in_t.at[rows],
-            send_sem=t_send.at[g],
-            recv_sem=t_recv.at[g],
+            send_sem=t_send.at[0],
+            recv_sem=t_recv.at[0],
             device_id=sibling,
             device_id_type=MESH,
         )
         copy.start()
-        t_copies.append(copy)
-        if g == 0:
-            pltpu.make_async_copy(sloc.at[c], sidx.at[pl.ds(row, 1)], i_recv.at[0]).start()
-            for k in range(1, rows_all):
-                copy = pltpu.make_async_remote_copy(
-                    src_ref=sloc.at[lax.rem(row + k, 2)],
-                    dst_ref=sidx.at[pl.ds(row, 1)],
-                    send_sem=i_send.at[k - 1],
-                    recv_sem=i_recv.at[0],
-                    device_id=(other_row(k), col),
-                    device_id_type=MESH,
-                )
-                copy.start()
-                sent.append(copy)
-    sent += t_copies
 
     def transform(ref):
         def body(i, _):
@@ -264,7 +265,7 @@
 
     transform(own)
 
-    pltpu.make_async_copy(sidx, sidx, i_recv.at[0]).wait()
+    arrived(sidx, i_recv.at[0])
     nb = rows_all
     index = sidx[...].astype(F32)
     if nb < 128:
@@ -272,8 +273,7 @@
     negative = lax.population_count(lane & row) & 1
     table[...] = (index.T.astype(jnp.int32) + 128 * negative).reshape(PAIRS, 8, 128)
 
-    for copy in t_copies:
-        copy.wait_recv()
+    arrived(in_t, t_recv.at[0])
     transform(in_t)
 
     lower = lax.broadcasted_iota(jnp.int32, (chips * 16, 128), 0) % 8 < 4
@@ -322,10 +322,9 @@
         if pairs % 2:
             one(first_pair + pairs - 1, pairs - 1, signs0)
         me, n, device = axes[axis]
-        stages[number, 1] = Stage(me, n, longer, 0, q, r1, s1, v1, device, sent)
+        stages[number, 1] = Stage(me, n, longer, 0, q, r1, s1, v1, device)
 
     scale = float(8192 * nb) ** (-0.5)
-    x_copies = []
 
     def finish(number):
         here = pl.ds(firsts[number], PARTS[number][1])
@@ -335,38 +334,38 @@
             lanes = slice(64 * h, 64 * h + 64)
             packed[h, here] = jnp.concatenate([value[0, :, :, lanes], value[1, :, :, lanes]], axis=2)
 
-        def send(slot, source, target, device):
+        def send(source, target, device):
             copy = pltpu.make_async_remote_copy(
                 src_ref=source,
                 dst_ref=target,
-                send_sem=x_send.at[slot, number],
-                recv_sem=x_recv.at[slot, number],
+                send_sem=x_send.at[number],
+                recv_sem=x_recv.at[number],
                 device_id=device,
                 device_id_type=MESH,
             )
             copy.start()
-            x_copies.append((number, copy))
-            sent.append(copy)
-
-        send(0, sk.at[:, here], beside_sk.at[:, here], sibling)
-        for k in range(1, nx):
-            send(2 * k - 1, packed.at[c, here], xg.at[k, 0, here], (row, other_col(k)))
-            send(2 * k, packed.at[other, here], xg.at[k, 1, here], (beside, other_col(k)))
+
+        for k in far_first(nx):
+            send(packed.at[c, here], xg.at[k, 0, here], (row, other_col(k)))
+            send(packed.at[other, here], xg.at[k, 1, here], (beside, other_col(k)))
+        send(sk.at[:, here], beside_sk.at[:, here], sibling)
 
     gr = nx * 128 // nb
     per_x = rows_all // nx
     group = per_x // 2
     dims = (((0,), (0,)), ((), ()))
 
+    def x_bytes(number):
+        return xg.at[:, :, pl.ds(firsts[number], PARTS[number][1])]
+
     def rows_of(get, numbers):
         return jnp.concatenate(
             [get(pl.ds(firsts[number], PARTS[number][1])).reshape(-1, 128) for number in numbers], axis=0
         )
 
     def gram(numbers, begin):
-        for number, copy in x_copies:
-            if number in numbers:
-                copy.wait_recv()
+        for number in numbers:
+            arrived(x_bytes(number), x_recv.at[number])
         near, far = [], []
         for core, ref in enumerate((sk, beside_sk)):
             near.append(
@@ -408,8 +407,12 @@
         q, r1, f, r2, s1, v1, s2, v2 = part_refs[8 * number : 8 * number + 8]
         f[...] = stages[number, 1].total()
         me, n, device = axes["y" if axis == "z" else "z"]
-        stages[number, 2] = Stage(me, n, longer, direct, f, r2, s2, v2, device, sent)
+        stages[number, 2] = Stage(me, n, longer, direct, f, r2, s2, v2, device)
     gram(done[:-LATE], True)
+    arrived(sidx.at[pl.ds(0, rows_all - 1)], i_send.at[0])
+    arrived(in_t, t_send.at[0])
+    for stage in stages.values():
+        stage.wait_sends()
     gram(done[-LATE:], False)
 
     in_half = lax.rem(row, per_x)
@@ -421,15 +424,15 @@
         return pltpu.make_async_remote_copy(
             src_ref=gbuf.at[t],
             dst_ref=g2.at[chip],
-            send_sem=h_send.at[k],
+            send_sem=h_send.at[0],
             recv_sem=h_recv.at[0],
             device_id=(t // group * per_x + c * group + lax.rem(t, group), col),
             device_id_type=MESH,
         )
 
     blocks = [to_target(k) for k in range(chips)]
-    for copy in blocks[1:]:
-        copy.start()
+    for k in far_first(chips):
+        blocks[k].start()
     pl.when(jnp.logical_not(here_too))(blocks[0].start)
 
     own_block = pltpu.make_async_copy(gbuf.at[first_block], g2.at[chip], h_recv.at[0])
@@ -437,12 +440,18 @@
 
     sk_out[c] = sk[c]
     sk_out[other] = beside_sk[c]
-    for copy in sent:
-        copy.wait_send()
-    for copy in blocks[1:]:
-        copy.wait_send()
-    pl.when(jnp.logical_not(here_too))(blocks[0].wait_send)
-    pltpu.make_async_copy(g2, g2, h_recv.at[0]).wait()
+    for number in range(len(PARTS)):
+        arrived(x_bytes(number), x_send.at[number])
+
+    @pl.when(here_too)
+    def _():
+        arrived(g2.at[pl.ds(0, chips - 1)], h_send.at[0])
+
+    @pl.when(jnp.logical_not(here_too))
+    def _():
+        arrived(g2, h_send.at[0])
+
+    arrived(g2, h_recv.at[0])
     g_out[...] = jnp.sum(g2[...], axis=0) * (1.0 / float(256 * nb))
 
 
@@ -469,27 +478,27 @@
         vm((nx, 2, PAIRS, 8, 128), F32),
         vm((chips, gr, 128), F32),
         vm((chips, gr, 128), F32),
-        dma((2 * CHUNKS + 2,)),
-        dma((CHUNKS,)),
-        dma((CHUNKS,)),
-        dma((2 * chips - 1,)),
+        dma((CHUNKS + 2,)),
         dma((1,)),
-        dma((2 * nx - 1, len(PARTS))),
-        dma((2 * nx - 1, len(PARTS))),
-        dma((chips,)),
+        dma((1,)),
+        dma((1,)),
+        dma((1,)),
+        dma((len(PARTS),)),
+        dma((len(PARTS),)),
+        dma((1,)),
         dma((1,)),
     ]
-    for axis, pairs, _, _ in PARTS:
+    for axis, pairs, _, scheme in PARTS:
         n1, n2 = (NZ, NY) if axis == "z" else (NY, NZ)
         scratch += [
             vm((n1, n2, pairs, 2, 8, 128), F32),
             vm((n1 - 1, n2, pairs, 2, 8, 128), F32),
             vm((n2, pairs, 2, 8, 128), F32),
             vm((n2 - 1, pairs, 2, 8, 128), F32),
+            dma((1,)),
             dma((n1 - 1,)),
-            dma((n1 - 1,)),
-            dma((n2 - 1,)),
-            dma((n2 - 1,)),
+            dma((1,)),
+            dma((2 if scheme else n2 - 1,)),
         ]
     sketch, gram = pl.pallas_call(
         functools.partial(kernel, nx),

time: 67 us -> 64 us (0.955)
  Pallas kernels: 65 us -> 62 us
    pallas_call x1, Pallas kernels: 65 us -> 62 us  [on_device(): pl.pallas_call(functools.partial(kernel, nx), out_shape=(jax.ShapeDtypeSt...]
where the time goes in v4:
time: 64 us; the launch traced here: 63.9 us
  Pallas kernels  62 us (97%)
  local copies, waits for them, and re-layouts  1.25 us (2%)
  between operations  0.64 us (1%)
    pallas_call x1, Pallas kernels, on_device(): pl.pallas_call(functools.partial(kernel, nx), out_shape=(jax.ShapeDtypeSt...  62 us

profile of v4, /device:TPU:1, one launch (start us, length us, event | category | flops | bytes accessed | tf_op | source)
XLA Modules:
  0.0 63.9 jit_solution(1556639519514466723)
XLA Ops:
  0.6 62.0 %shard_map.50 = (f32[2,16,8,128]{3,2,1,0:T(8,128)S(1)}, f32[8,128]{1,0:T(8,128)S(1)}) custom-call(bf16[64,128,128]{2,1,0:T(8,128)(2,1)} %bitcast.4, s32[64,128]{1,0:T(8,128)} %bitcast.5, s32[1,256]{1,0:T(1,128)} %smp_hbm.1), custom_call_target="tpu_custom_call" | custom-call | tf_op jit(solution)/shard_map/pallas_call | solution.py:503
  62.6 0.7 %copy.7 = f32[256,128]{1,0:T(8,128)} copy(f32[256,128]{1,0:T(8,128)S(1)} %bitcast.3) | data formatting | bytes 262144
  63.3 0.6 copy.8

commit v5 on v4

--- a/solution.py
+++ b/solution.py
@@ -14,9 +14,9 @@
 PAIRS = 16
 LATE = 2
 PARTS = (
+    ("z", 2, 0, 1),
     ("z", 2, 1, 1),
     ("y", 2, 0, 2),
-    ("z", 2, 0, 1),
     ("y", 2, 1, 2),
     ("z", 2, 0, 1),
     ("z", 2, 1, 1),
@@ -24,13 +24,13 @@
     ("y", 2, 1, 2),
 )
 ORDER = (
-    (0, 1, 0, 1), (0, 1, 1, 1), (2, 1, 0, 1), (2, 1, 1, 1), (1, 1, 0, 1), (1, 1, 1, 1), (4, 1, 0, 1), (4, 1, 1, 1),
-    (5, 1, 0, 1), (5, 1, 1, 1), (3, 1, 0, 1), (3, 1, 1, 1), (0, 1, 0, 2), (0, 1, 1, 2), (2, 1, 0, 2), (2, 1, 1, 2),
+    (0, 1, 0, 1), (0, 1, 1, 1), (1, 1, 0, 1), (1, 1, 1, 1), (2, 1, 0, 1), (2, 1, 1, 1), (4, 1, 0, 1), (4, 1, 1, 1),
+    (5, 1, 0, 1), (5, 1, 1, 1), (3, 1, 0, 1), (3, 1, 1, 1), (0, 1, 0, 2), (0, 1, 1, 2), (1, 1, 0, 2), (1, 1, 1, 2),
     (6, 1, 0, 1), (6, 1, 1, 1), (4, 1, 0, 2), (4, 1, 1, 2), (5, 1, 0, 2), (5, 1, 1, 2), (7, 1, 0, 1), (7, 1, 1, 1),
-    (0, 1, 0, 3), (0, 1, 1, 3), (2, 1, 0, 3), (2, 1, 1, 3), (1, 1, 0, 2), (3, 1, 1, 2), (4, 1, 0, 3), (4, 1, 1, 3),
-    (5, 1, 0, 3), (5, 1, 1, 3), (6, 1, 0, 2), (7, 1, 1, 2), (0, 1, 1, 4), (2, 1, 0, 4), (1, 2, 0, 1), (3, 2, 0, 1),
-    (5, 1, 1, 4), (4, 1, 0, 4), (0, 2, 0, 1), (2, 2, 0, 1), (6, 2, 0, 1), (7, 2, 0, 1), (1, 2, 0, 2), (3, 2, 0, 2),
-    (5, 2, 0, 1), (4, 2, 0, 1), (6, 2, 0, 2), (7, 2, 0, 2),
+    (0, 1, 0, 3), (0, 1, 1, 3), (1, 1, 0, 3), (1, 1, 1, 3), (2, 1, 0, 2), (3, 1, 1, 2), (4, 1, 0, 3), (4, 1, 1, 3),
+    (5, 1, 0, 3), (5, 1, 1, 3), (6, 1, 0, 2), (0, 1, 0, 4), (7, 1, 1, 2), (1, 1, 1, 4), (2, 2, 0, 1), (3, 2, 0, 1),
+    (4, 1, 0, 4), (5, 1, 1, 4), (0, 2, 0, 1), (1, 2, 0, 1), (6, 2, 0, 1), (7, 2, 0, 1), (2, 2, 0, 2), (3, 2, 0, 2),
+    (4, 2, 0, 1), (5, 2, 0, 1), (6, 2, 0, 2), (7, 2, 0, 2),
 )
 
 
@@ -148,7 +148,7 @@
 
 def kernel(
     nx, x_hbm, sgn_hbm, smp_hbm, sk_out, g_out,
-    x_v, sgn_ref, smp_ref, own, out_t, in_t, sloc, sidx, table, signs0, signs1, sk, beside_sk, packed, xg, gbuf, g2,
+    x_v, sgn_ref, smp_ref, own, out_t, in_t, sloc, sidx, table, signs0, signs1, high, low, sk, beside_sk, packed, xg, gbuf, g2,
     load_sem, t_send, t_recv, i_send, i_recv, x_send, x_recv, h_send, h_recv, *part_refs,
 ):
     row, col = lax.axis_index("row"), lax.axis_index("col")
@@ -264,6 +264,21 @@
         lax.fori_loop(0, 16, body, 0)
 
     transform(own)
+    arrived(in_t, t_recv.at[0])
+    transform(in_t)
+
+    def halve(p, _):
+        field = jnp.concatenate(
+            [
+                jnp.concatenate([own[2 * p], own[2 * p + 1]], axis=1),
+                jnp.concatenate([in_t[2 * p], in_t[2 * p + 1]], axis=1),
+            ],
+            axis=0,
+        )
+        high[p], low[p] = split(field)
+        return 0
+
+    lax.fori_loop(0, PAIRS, halve, 0)
 
     arrived(sidx, i_recv.at[0])
     nb = rows_all
@@ -272,9 +287,6 @@
         index = jnp.concatenate([index, jnp.zeros((128 - nb, 128), F32)], axis=0)
     negative = lax.population_count(lane & row) & 1
     table[...] = (index.T.astype(jnp.int32) + 128 * negative).reshape(PAIRS, 8, 128)
-
-    arrived(in_t, t_recv.at[0])
-    transform(in_t)
 
     lower = lax.broadcasted_iota(jnp.int32, (chips * 16, 128), 0) % 8 < 4
     place8 = lax.broadcasted_iota(jnp.int32, (8, 128), 1) + 128
@@ -298,16 +310,8 @@
                 here = pl.ds(place * 16, 16)
                 signs[here, :128] = jnp.concatenate(rows, axis=0).astype(BF16)
                 signs[here, 128:] = jnp.concatenate([rows[0], -rows[1]], axis=0).astype(BF16)
-            field = jnp.concatenate(
-                [
-                    jnp.concatenate([own[2 * p], own[2 * p + 1]], axis=1),
-                    jnp.concatenate([in_t[2 * p], in_t[2 * p + 1]], axis=1),
-                ],
-                axis=0,
-            )
-            high, low = split(field)
-            both = jnp.dot(signs[...], high, preferred_element_type=F32) + jnp.dot(
-                signs[...], low, preferred_element_type=F32
+            both = jnp.dot(signs[...], high[p], preferred_element_type=F32) + jnp.dot(
+                signs[...], low[p], preferred_element_type=F32
             )
             value = jnp.where(lower, both[:, :128], both[:, 128:])
             q[:, :, i] = value.reshape(n1, n2, 2, 8, 128)
@@ -472,6 +476,8 @@
         vm((PAIRS, 8, 128), jnp.int32),
         vm((chips * 16, 256), BF16),
         vm((chips * 16, 256), BF16),
+        vm((PAIRS, 256, 256), BF16),
+        vm((PAIRS, 256, 256), BF16),
         vm((2, PAIRS, 8, 128), F32),
         vm((2, PAIRS, 8, 128), F32),
         vm((2, PAIRS, 8, 128), F32),

time: 64 us -> 63.5 us (level)
  no operation moved by 1% of the time
where the time goes in v5:
time: 63.5 us; the launch traced here: 63.4 us
  Pallas kernels  61.5 us (97%)
  local copies, waits for them, and re-layouts  1.25 us (2%)
  between operations  0.64 us (1%)
    pallas_call x1, Pallas kernels, on_device(): pl.pallas_call(functools.partial(kernel, nx), out_shape=(jax.ShapeDtypeSt...  61.5 us

profile of v5, /device:TPU:1, one launch (start us, length us, event | category | flops | bytes accessed | tf_op | source)
XLA Modules:
  0.0 63.4 jit_solution(4067958407152733495)
XLA Ops:
  0.6 61.5 %shard_map.50 = (f32[2,16,8,128]{3,2,1,0:T(8,128)S(1)}, f32[8,128]{1,0:T(8,128)S(1)}) custom-call(bf16[64,128,128]{2,1,0:T(8,128)(2,1)} %bitcast.4, s32[64,128]{1,0:T(8,128)} %bitcast.5, s32[1,256]{1,0:T(1,128)} %smp_hbm.1), custom_call_target="tpu_custom_call" | custom-call | tf_op jit(solution)/shard_map/pallas_call | solution.py:509
  62.1 0.7 %copy.7 = f32[256,128]{1,0:T(8,128)} copy(f32[256,128]{1,0:T(8,128)S(1)} %bitcast.3) | data formatting | bytes 262144
  62.8 0.6 copy.8

commit v6 on v5

--- a/solution.py
+++ b/solution.py
@@ -342,8 +342,8 @@
             copy = pltpu.make_async_remote_copy(
                 src_ref=source,
                 dst_ref=target,
-                send_sem=x_send.at[number],
-                recv_sem=x_recv.at[number],
+                send_sem=x_send.at[0],
+                recv_sem=x_recv.at[0 if len(done) < len(PARTS) - LATE else 1],
                 device_id=device,
                 device_id_type=MESH,
             )
@@ -359,8 +359,8 @@
     group = per_x // 2
     dims = (((0,), (0,)), ((), ()))
 
-    def x_bytes(number):
-        return xg.at[:, :, pl.ds(firsts[number], PARTS[number][1])]
+    def x_bytes(numbers):
+        return xg.at[:, :, pl.ds(0, sum(PARTS[number][1] for number in numbers))]
 
     def rows_of(get, numbers):
         return jnp.concatenate(
@@ -368,8 +368,7 @@
         )
 
     def gram(numbers, begin):
-        for number in numbers:
-            arrived(x_bytes(number), x_recv.at[number])
+        arrived(x_bytes(numbers), x_recv.at[0 if begin else 1])
         near, far = [], []
         for core, ref in enumerate((sk, beside_sk)):
             near.append(
@@ -444,8 +443,7 @@
 
     sk_out[c] = sk[c]
     sk_out[other] = beside_sk[c]
-    for number in range(len(PARTS)):
-        arrived(x_bytes(number), x_send.at[number])
+    arrived(xg, x_send.at[0])
 
     @pl.when(here_too)
     def _():
@@ -489,8 +487,8 @@
         dma((1,)),
         dma((1,)),
         dma((1,)),
-        dma((len(PARTS),)),
-        dma((len(PARTS),)),
+        dma((1,)),
+        dma((2,)),
         dma((1,)),
         dma((1,)),
     ]
@@ -504,7 +502,7 @@
             dma((1,)),
             dma((n1 - 1,)),
             dma((1,)),
-            dma((2 if scheme else n2 - 1,)),
+            dma(((2 if n2 == 8 and scheme == 2 else 1) if scheme else n2 - 1,)),
         ]
     sketch, gram = pl.pallas_call(
         functools.partial(kernel, nx),

time: 63.5 us -> 63.3 us (level)
  no operation moved by 1% of the time
where the time goes in v6:
time: 63.3 us; the launch traced here: 63.2 us
  Pallas kernels  61.4 us (97%)
  local copies, waits for them, and re-layouts  1.25 us (2%)
  between operations  0.64 us (1%)
    pallas_call x1, Pallas kernels, on_device(): pl.pallas_call(functools.partial(kernel, nx), out_shape=(jax.ShapeDtypeSt...  61.4 us

profile of v6, /device:TPU:1, one launch (start us, length us, event | category | flops | bytes accessed | tf_op | source)
XLA Modules:
  0.0 63.2 jit_solution(6713102733041996498)
XLA Ops:
  0.6 61.4 %shard_map.50 = (f32[2,16,8,128]{3,2,1,0:T(8,128)S(1)}, f32[8,128]{1,0:T(8,128)S(1)}) custom-call(bf16[64,128,128]{2,1,0:T(8,128)(2,1)} %bitcast.4, s32[64,128]{1,0:T(8,128)} %bitcast.5, s32[1,256]{1,0:T(1,128)} %smp_hbm.1), custom_call_target="tpu_custom_call" | custom-call | tf_op jit(solution)/shard_map/pallas_call | solution.py:507
  62.0 0.7 %copy.7 = f32[256,128]{1,0:T(8,128)} copy(f32[256,128]{1,0:T(8,128)S(1)} %bitcast.3) | data formatting | bytes 262144
  62.6 0.6 copy.8
